TPU v7x, 32 devices: a whole 2x2x4 slice. The times are simulated.
32 devices in a mesh: dp: 4 (over z), ctx: 4 (over y, x), tp: 2 (over core).
Axes of the slice: x: 2, y: 2, z: 4, core: 2. Of those that a mesh axis runs over, the one named last changes fastest.
Arguments:
- tokens: bfloat16 [8, 1024, 1024], P('dp', 'ctx'), may hold values from -6 to 6
- segment_ids: int32 [8, 1024], P('dp', 'ctx'), may hold values from 0 to 3, as said below
- out_grad: bfloat16 [8, 1024, 1024], P('dp', 'ctx'), may hold values from -6 to 6
- attn_gain: bfloat16 [1024], P(('dp', 'ctx')), may hold values from 0.5 to 1.5
- ffn_gain: bfloat16 [1024], P(('dp', 'ctx')), may hold values from 0.5 to 1.5
- attention_input_weight: bfloat16 [1024, 768], P(('dp', 'ctx'), 'tp'), may hold values from -0.1875 to 0.1875
- state_space_input_weight: bfloat16 [1024, 3072], P(('dp', 'ctx'), 'tp'), may hold values from -0.1875 to 0.1875
- scan_input_weight: bfloat16 [1024, 280], P(('dp', 'ctx')), may hold values from -0.1875 to 0.1875
- mixer_output_weight: bfloat16 [1024, 2048], P(('dp', 'ctx'), 'tp'), may hold values from -0.125 to 0.125
- gate_up_weight: bfloat16 [1024, 4096], P(('dp', 'ctx'), 'tp'), may hold values from -0.1875 to 0.1875
- down_weight_matrix: bfloat16 [1024, 2048], P(('dp', 'ctx'), 'tp'), may hold values from -0.125 to 0.125
- log_decay: float32 [24], P('tp'), may hold values from -4.6 to 0
- step_bias: float32 [24], P('tp'), may hold values from -6.9 to -2.3
- skip_gain: float32 [24], P('tp'), may hold values from 0.5 to 1.5
- conv_x_weight: float32 [4, 1536], P(None, 'tp'), may hold values from -3 to 3
- conv_x_bias: float32 [1536], P('tp'), may hold values from -0.5 to 0.5
- conv_bc_weight: float32 [4, 256], replicated, may hold values from -3 to 3
- conv_bc_bias: float32 [256], replicated, may hold values from -0.5 to 0.5
Outputs:
- layer_out: bfloat16 [8, 1024, 1024], P('dp', 'ctx')
- tokens_grad: float32 [8, 1024, 1024], P('dp', 'ctx')
- attn_gain_grad: float32 [1024], P(('dp', 'ctx'))
- ffn_gain_grad: float32 [1024], P(('dp', 'ctx'))
- attn_in_grad: float32 [1024, 768], P(('dp', 'ctx'), 'tp')
- ssm_in_grad: float32 [1024, 3072], P(('dp', 'ctx'), 'tp')
- scan_in_grad: float32 [1024, 280], P(('dp', 'ctx'))
- mixer_out_grad: float32 [1024, 2048], P(('dp', 'ctx'), 'tp')
- gate_up_grad: float32 [1024, 4096], P(('dp', 'ctx'), 'tp')
- down_proj_grad: float32 [1024, 2048], P(('dp', 'ctx'), 'tp')
- log_decay_grad: float32 [24], P('tp')
- step_bias_grad: float32 [24], P('tp')
- skip_gain_grad: float32 [24], P('tp')
- conv_x_weight_grad: float32 [4, 1536], P(None, 'tp')
- conv_x_bias_grad: float32 [1536], P('tp')
- conv_bc_weight_grad: float32 [4, 256], replicated
- conv_bc_bias_grad: float32 [256], replicated
Inputs may be any that keep to these rules, and one draw needn't show every extreme that they name: `segment_ids`: in each sequence the ids start at 0, never fall, and rise by one at a boundary; one document starts within the first 256 positions and ends within the last 256.
All inputs are finite; a program needn't handle non-finite values.
Results may differ from a plain program's by a relative error of at most 0.018.
Values may be sent and summed in bfloat16 or wider, within the bound.
A program may use at most 128 MiB of HBM per device.

v0:
```python
import jax
import jax.numpy as jnp
from jax import lax
from jax.sharding import PartitionSpec as P

HEADS = 8
HEAD_SIZE = 64
M_HEADS = 24
M_HEAD = 64
STATE = 128
FF = 2048


epsilon = 1e-05
rope_base = 100000000000.0
big_negative = -1e30


def carried_in(array, axis, combine, identity):
    count, mine = (lax.axis_size(axis), lax.axis_index(axis))
    everything = jax.tree.map(
        lambda part, kind: lax.all_gather(part.astype(kind), axis),
        array,
        (jnp.bfloat16, jnp.bfloat16, jnp.bfloat16, jnp.bfloat16),
    )
    start = jax.tree.map(
        lambda part, zero: jnp.broadcast_to(jnp.asarray(zero, part.dtype), part.shape),
        array,
        identity,
    )

    def step(k, before):
        reached = k < mine
        new = combine(
            before, jax.tree.map(lambda part, own: part[k].astype(own.dtype), everything, array)
        )
        return jax.tree.map(lambda a, b: jnp.where(reached, a, b), new, before)

    return lax.fori_loop(0, count, step, start)


def prefix(array, axis, join, neutral):
    count = lax.axis_size(axis)
    place = lax.axis_index(axis)
    ahead = count - 1 - place
    gathered = jax.tree.map(
        lambda a, kind: lax.all_gather(a.astype(kind), axis), array, (jnp.bfloat16, jnp.bfloat16)
    )
    state = jax.tree.map(lambda a, e: jnp.zeros_like(a) + jnp.asarray(e, a.dtype), array, neutral)

    def one(step, state):
        source = count - 1 - step
        return join(
            state,
            jax.tree.map(
                lambda a, own: lax.dynamic_index_in_dim(a, source, 0, False).astype(own.dtype),
                gathered,
                array,
            ),
        )

    return lax.fori_loop(0, ahead, one, state)


def shifted(value, axis, steps):
    count = lax.axis_size(axis)
    initial, last = (max(0, -steps), min(count, count - steps))
    return lax.ppermute(value, axis, [(source, source + steps) for source in range(initial, last)])


def rms_scale(values):
    return lax.rsqrt(jnp.mean(values * values, -1, keepdims=True) + epsilon)


def norm_back(grad_out, normed, row_scale, gain_vec):
    grad_normed = grad_out * gain_vec
    return row_scale * (grad_normed - normed * jnp.mean(grad_normed * normed, -1, keepdims=True))


def rotate(values, cosine, sine_part):
    half_dim = values.shape[-1] // 2
    front, back_half = (values[..., :half_dim], values[..., half_dim:])
    return jnp.concatenate(
        [front * cosine - back_half * sine_part, back_half * cosine + front * sine_part], -1
    )


def silu_slope(values):
    sigmoid_vals = jax.nn.sigmoid(values)
    return sigmoid_vals * (1.0 + values * (1.0 - sigmoid_vals))


def conv_forward(extended, own_seg, seg_before_ext, weight, bias, count):
    reach = weight.shape[0] - 1
    total = bias
    for lag in range(reach + 1):
        start = reach - lag
        same = (seg_before_ext[:, start : start + count] == own_seg).astype(jnp.float32)
        total = total + weight[lag] * extended[:, start : start + count] * same[..., None]
    return total


def conv_backward(grad_ext, extended, own_seg, seg_before_ext, seg_after_ext, weight, count):
    reach = weight.shape[0] - 1
    own_grad = grad_ext[:, :count]
    input_grad = jnp.zeros_like(own_grad)
    tap_grads = []
    for lag in range(reach + 1):
        ahead = (seg_after_ext[:, lag : lag + count] == own_seg).astype(jnp.float32)
        input_grad = input_grad + weight[lag] * grad_ext[:, lag : lag + count] * ahead[..., None]
        start = reach - lag
        behind = (seg_before_ext[:, start : start + count] == own_seg).astype(jnp.float32)
        tap_grads.append(
            jnp.sum(own_grad * extended[:, start : start + count] * behind[..., None], (0, 1))
        )
    return (input_grad, jnp.stack(tap_grads), jnp.sum(own_grad, (0, 1)))


def link_states(early_part, late_part):
    early_first, early_last, early_gate, early_state = early_part
    late_first, late_last, late_gate, late_state = late_part
    joined = ((early_last == late_first) | (early_last < -0.5) | (late_first < -0.5)).astype(
        jnp.float32
    )
    first_seg = jnp.where(early_first < -0.5, late_first, early_first)
    last_seg = jnp.where(late_last < -0.5, early_last, late_last)
    passing = late_gate * joined[:, None]
    return (
        first_seg,
        last_seg,
        early_gate * passing,
        late_state + passing[:, :, None, None] * early_state,
    )


def link_grads(early_part, late_part):
    early_gate, early_grad = early_part
    late_gate, late_grad = late_part
    return (early_gate * late_gate, late_grad + late_gate[:, :, None, None] * early_grad)


def per_device(
    tokens,
    segment_ids,
    out_grad,
    attn_gain,
    ffn_gain,
    attention_input_weight,
    state_space_input_weight,
    scan_input_weight,
    mixer_output_weight,
    gate_up_weight,
    down_weight_matrix,
    log_decay,
    step_bias,
    skip_gain,
    conv_x_weight,
    conv_x_bias,
    conv_bc_weight,
    conv_bc_bias,
):
    single_layer = jnp.float32
    narrow_slice = jnp.bfloat16
    tp_count = lax.axis_size("tp")
    ctx_count = lax.axis_size("ctx")
    tp_index = lax.axis_index("tp")
    ctx_index = lax.axis_index("ctx")
    sequences, tok_count, model_width = tokens.shape
    head_count = HEADS // tp_count
    mamba_count = M_HEADS // tp_count
    query_width = head_count * HEAD_SIZE
    mamba_width = mamba_count * M_HEAD
    ffn_width = FF // tp_count
    row_count = tok_count * head_count
    score_scale = HEAD_SIZE ** (-0.5)
    reach = conv_x_weight.shape[0] - 1
    full_qkv, full_zx, full_bcd, full_mix, full_gu, full_down, gain_one, gain_two = (
        lax.all_gather(attention_input_weight, ("dp", "ctx"), axis=0, tiled=True),
        lax.all_gather(state_space_input_weight, ("dp", "ctx"), axis=0, tiled=True),
        lax.all_gather(scan_input_weight, ("dp", "ctx"), axis=0, tiled=True),
        lax.all_gather(mixer_output_weight, ("dp", "ctx"), axis=0, tiled=True),
        lax.all_gather(gate_up_weight, ("dp", "ctx"), axis=0, tiled=True),
        lax.all_gather(down_weight_matrix, ("dp", "ctx"), axis=0, tiled=True),
        lax.all_gather(attn_gain, ("dp", "ctx"), axis=0, tiled=True),
        lax.all_gather(ffn_gain, ("dp", "ctx"), axis=0, tiled=True),
    )
    gain_one = gain_one.astype(single_layer)
    gain_two = gain_two.astype(single_layer)
    layer_inputs = tokens.astype(single_layer)
    first_scale = rms_scale(layer_inputs)
    first_normed = layer_inputs * first_scale
    first_norm_slice = (first_normed * gain_one).astype(narrow_slice)
    qkv_vals = jnp.einsum(
        "btd,dc->btc", first_norm_slice, full_qkv, preferred_element_type=single_layer
    )
    gate_input_values = jnp.einsum(
        "btd,dc->btc", first_norm_slice, full_zx, preferred_element_type=single_layer
    )
    scan_input_values = jnp.einsum(
        "btd,dc->btc", first_norm_slice, full_bcd, preferred_element_type=single_layer
    )
    half_dim = HEAD_SIZE // 2
    frequency = rope_base ** (-jnp.arange(half_dim, dtype=single_layer) * 2.0 / HEAD_SIZE)
    positions = (ctx_index * tok_count + jnp.arange(tok_count, dtype=jnp.int32)).astype(
        single_layer
    )
    angles = positions[:, None] * frequency[None, :]
    cosine, sine_part = (jnp.cos(angles), jnp.sin(angles))
    query_rot = rotate(
        qkv_vals[..., :query_width].reshape(sequences, tok_count, head_count, HEAD_SIZE),
        cosine[None, :, None],
        sine_part[None, :, None],
    )
    query_slice = query_rot.astype(narrow_slice).reshape(sequences, row_count, HEAD_SIZE)
    key_rot = rotate(
        qkv_vals[..., query_width : query_width + HEAD_SIZE], cosine[None], sine_part[None]
    )
    key_value = jnp.concatenate([key_rot, qkv_vals[..., query_width + HEAD_SIZE :]], -1).astype(
        narrow_slice
    )
    seg_float = segment_ids.astype(single_layer)
    conv_x_in = gate_input_values[..., mamba_width:].astype(narrow_slice)
    conv_bc_in = scan_input_values[..., : 2 * STATE].astype(narrow_slice)
    all_kv, all_seg, tails_x, tails_bc = (
        lax.all_gather(key_value, "ctx", axis=1, tiled=True),
        lax.all_gather(seg_float.astype(narrow_slice), "ctx", axis=1, tiled=True),
        lax.all_gather(conv_x_in[:, tok_count - reach :], "ctx", axis=1, tiled=True),
        lax.all_gather(conv_bc_in[:, tok_count - reach :], "ctx", axis=1, tiled=True),
    )
    full_len = all_kv.shape[1]
    seg_all = all_seg.astype(single_layer)
    has_prev = ctx_index > 0
    has_next = ctx_index < ctx_count - 1
    prev_index = jnp.maximum(ctx_index - 1, 0)
    prev_x = lax.dynamic_slice_in_dim(tails_x, prev_index * reach, reach, 1)
    prev_bc = lax.dynamic_slice_in_dim(tails_bc, prev_index * reach, reach, 1)
    prev_x = jnp.where(has_prev, prev_x, jnp.zeros_like(prev_x))
    prev_bc = jnp.where(has_prev, prev_bc, jnp.zeros_like(prev_bc))
    prev_seg = lax.dynamic_slice_in_dim(
        seg_all, jnp.maximum(ctx_index * tok_count - reach, 0), reach, 1
    )
    prev_seg = jnp.where(has_prev, prev_seg, -jnp.ones_like(prev_seg))
    next_seg = lax.dynamic_slice_in_dim(
        seg_all, jnp.minimum((ctx_index + 1) * tok_count, full_len - reach), reach, 1
    )
    next_seg = jnp.where(has_next, next_seg, -jnp.ones_like(next_seg))
    seg_before_ext = jnp.concatenate([prev_seg, seg_float], 1)
    seg_after_ext = jnp.concatenate([seg_float, next_seg], 1)
    ext_x = jnp.concatenate([prev_x, conv_x_in], 1).astype(single_layer)
    ext_bc = jnp.concatenate([prev_bc, conv_bc_in], 1).astype(single_layer)
    conv_x_pre = conv_forward(
        ext_x, seg_float, seg_before_ext, conv_x_weight, conv_x_bias, tok_count
    )
    conv_bc_pre = conv_forward(
        ext_bc, seg_float, seg_before_ext, conv_bc_weight, conv_bc_bias, tok_count
    )
    block_len = min(512, full_len)
    needed = ((ctx_index + 1) * tok_count + block_len - 1) // block_len
    row_pos = ctx_index * tok_count + jnp.arange(row_count, dtype=jnp.int32) // head_count
    row_seg = jnp.repeat(seg_float, head_count, axis=1)

    def block_scores(block_index):
        key_start = block_index * block_len
        key_block_rows = lax.dynamic_slice_in_dim(all_kv, key_start, block_len, 1)
        key_seg = lax.dynamic_slice_in_dim(all_seg, key_start, block_len, 1).astype(single_layer)
        key_pos = key_start + jnp.arange(block_len, dtype=jnp.int32)
        allowed = (key_pos[None, None, :] <= row_pos[None, :, None]) & (
            key_seg[:, None, :] == row_seg[:, :, None]
        )
        raw_scores = (
            jnp.einsum(
                "nwl,nol->nwo",
                query_slice,
                key_block_rows[..., :HEAD_SIZE],
                preferred_element_type=single_layer,
            )
            * score_scale
        )
        return (jnp.where(allowed, raw_scores, big_negative), allowed, key_block_rows)

    def peak_step(block_index, carry):
        row_peak, row_total = carry
        scores, allowed, key_block_rows = block_scores(block_index)
        new_peak = jnp.maximum(row_peak, jnp.max(scores, -1))
        kept = jnp.where(allowed, jnp.exp(scores - new_peak[..., None]), 0.0)
        return (new_peak, row_total * jnp.exp(row_peak - new_peak) + jnp.sum(kept, -1))

    row_peak, row_total = lax.fori_loop(
        0,
        needed,
        peak_step,
        (
            jnp.full((sequences, row_count), big_negative, single_layer),
            jnp.zeros((sequences, row_count), single_layer),
        ),
    )
    log_total = row_peak + jnp.log(row_total)

    def value_step(block_index, accum):
        scores, allowed, key_block_rows = block_scores(block_index)
        probability_slice = jnp.where(allowed, jnp.exp(scores - log_total[..., None]), 0.0).astype(
            narrow_slice
        )
        return accum + jnp.einsum(
            "znw,zwt->znt",
            probability_slice,
            key_block_rows[..., HEAD_SIZE:],
            preferred_element_type=single_layer,
        )

    attn_vals = lax.fori_loop(
        0, needed, value_step, jnp.zeros((sequences, row_count, HEAD_SIZE), single_layer)
    )
    attn_low = attn_vals.astype(narrow_slice).reshape(sequences, tok_count, query_width)
    z_vals = gate_input_values[..., :mamba_width].reshape(sequences, tok_count, mamba_count, M_HEAD)
    xs_low = (
        jax.nn.silu(conv_x_pre)
        .astype(narrow_slice)
        .reshape(sequences, tok_count, mamba_count, M_HEAD)
    )
    xs_vals = xs_low.astype(single_layer)
    bc_low = jax.nn.silu(conv_bc_pre).astype(narrow_slice)
    b_low = bc_low[..., :STATE]
    c_low = bc_low[..., STATE:]
    step_raw = lax.dynamic_slice_in_dim(
        scan_input_values, 2 * STATE + tp_index * mamba_count, mamba_count, 2
    )
    step_size = jax.nn.softplus(step_raw + step_bias)
    decay_rate = jnp.exp(log_decay)
    log_step = -decay_rate * step_size
    cumulative = jnp.cumsum(log_step, 1)
    cum_heads = jnp.moveaxis(cumulative, 2, 1)
    step_heads = jnp.moveaxis(step_size, 2, 1)
    causal = (
        jnp.arange(tok_count, dtype=jnp.int32)[:, None]
        >= jnp.arange(tok_count, dtype=jnp.int32)[None, :]
    )
    same_doc = (seg_float[:, :, None] == seg_float[:, None, :]) & causal[None]
    allowed_heads = same_doc[:, None]
    gap = cum_heads[:, :, :, None] - cum_heads[:, :, None, :]
    expo = jnp.where(allowed_heads, jnp.exp(jnp.where(allowed_heads, gap, 0.0)), 0.0)
    pair = jnp.einsum("btn,bsn->bts", c_low, b_low, preferred_element_type=single_layer)
    mix_matrix = (expo * pair[:, None] * step_heads[:, :, None, :]).astype(narrow_slice)
    intra_term = jnp.einsum(
        "bhts,bshp->bthp", mix_matrix, xs_low, preferred_element_type=single_layer
    )
    end_decay = (
        jnp.exp(cumulative[:, -1:] - cumulative)
        * (seg_float == seg_float[:, -1:]).astype(single_layer)[:, :, None]
    )
    end_weight = end_decay * step_size
    weighted_low = (xs_vals * end_weight[..., None]).astype(narrow_slice)
    local_state = jnp.einsum(
        "bshp,bsn->bhpn", weighted_low, b_low, preferred_element_type=single_layer
    )
    block_gate = (
        jnp.exp(cumulative[:, -1])
        * (seg_float[:, 0] == seg_float[:, -1]).astype(single_layer)[:, None]
    )
    negative = -jnp.ones((sequences,), single_layer)
    identity = (negative, negative, jnp.ones_like(block_gate), jnp.zeros_like(local_state))
    _, seg_before, _, state_before = carried_in(
        (seg_float[:, 0], seg_float[:, -1], block_gate, local_state), "ctx", link_states, identity
    )
    state_low = state_before.astype(narrow_slice)
    inter_term = jnp.einsum("btn,bhpn->bthp", c_low, state_low, preferred_element_type=single_layer)
    entry_decay = (
        jnp.exp(cumulative) * (seg_float == seg_before[:, None]).astype(single_layer)[:, :, None]
    )
    ssm_vals = intra_term + entry_decay[..., None] * inter_term
    mamba_y = ssm_vals + skip_gain[:, None] * xs_vals
    mamba_out = mamba_y * jax.nn.silu(z_vals)
    mixer_slice = jnp.concatenate(
        [mamba_out.reshape(sequences, tok_count, mamba_width).astype(narrow_slice), attn_low], -1
    )
    mix_part = jnp.einsum("btc,dc->btd", mixer_slice, full_mix, preferred_element_type=single_layer)
    middle_state = layer_inputs + lax.psum(mix_part.astype(jnp.bfloat16), "tp").astype(jnp.float32)
    second_scale = rms_scale(middle_state)
    second_normed = middle_state * second_scale
    second_norm_slice = (second_normed * gain_two).astype(narrow_slice)
    gu_vals = jnp.einsum(
        "btd,dc->btc", second_norm_slice, full_gu, preferred_element_type=single_layer
    )
    gate_values, up_vals = (gu_vals[..., :ffn_width], gu_vals[..., ffn_width:])
    activation_slice = (jax.nn.silu(gate_values) * up_vals).astype(narrow_slice)
    ffn_part = jnp.einsum(
        "btc,dc->btd", activation_slice, full_down, preferred_element_type=single_layer
    )
    layer_out = (
        middle_state + lax.psum(ffn_part.astype(jnp.bfloat16), "tp").astype(jnp.float32)
    ).astype(narrow_slice)
    cotangent = out_grad.astype(single_layer)
    grad_down_w = jnp.einsum(
        "btd,btc->dc", out_grad, activation_slice, preferred_element_type=single_layer
    )
    grad_act = jnp.einsum("btd,dc->btc", out_grad, full_down, preferred_element_type=single_layer)
    grad_gu_low = jnp.concatenate(
        [grad_act * up_vals * silu_slope(gate_values), grad_act * jax.nn.silu(gate_values)], -1
    ).astype(narrow_slice)
    grad_gu_w = jnp.einsum(
        "btd,btc->dc", second_norm_slice, grad_gu_low, preferred_element_type=single_layer
    )
    second_part = jnp.einsum(
        "btc,dc->btd", grad_gu_low, full_gu, preferred_element_type=single_layer
    )
    grad_second = lax.psum(second_part.astype(jnp.bfloat16), "tp").astype(jnp.float32)
    grad_gain_two = jnp.sum(grad_second * second_normed, (0, 1))
    grad_middle = cotangent + norm_back(grad_second, second_normed, second_scale, gain_two)
    grad_mix_low = grad_middle.astype(narrow_slice)
    grad_mix_w = jnp.einsum(
        "btd,btc->dc", grad_mix_low, mixer_slice, preferred_element_type=single_layer
    )
    grad_cat = jnp.einsum(
        "btd,dc->btc", grad_mix_low, full_mix, preferred_element_type=single_layer
    )
    grad_mamba = grad_cat[..., :mamba_width].reshape(sequences, tok_count, mamba_count, M_HEAD)
    attention_gradient_slice = (
        grad_cat[..., mamba_width:].astype(narrow_slice).reshape(sequences, row_count, HEAD_SIZE)
    )
    delta = jnp.sum(attention_gradient_slice.astype(single_layer) * attn_vals, -1)

    def grad_step(block_index, carry):
        grad_query, grad_kv = carry
        scores, allowed, key_block_rows = block_scores(block_index)
        attention_probabilities = jnp.where(allowed, jnp.exp(scores - log_total[..., None]), 0.0)
        grad_probs = jnp.einsum(
            "nwl,nol->nwo",
            attention_gradient_slice,
            key_block_rows[..., HEAD_SIZE:],
            preferred_element_type=single_layer,
        )
        score_gradient = (
            attention_probabilities * (grad_probs - delta[..., None]) * score_scale
        ).astype(narrow_slice)
        grad_query = grad_query + jnp.einsum(
            "znw,zwt->znt",
            score_gradient,
            key_block_rows[..., :HEAD_SIZE],
            preferred_element_type=single_layer,
        )
        grad_keys = jnp.einsum(
            "pni,pnx->pix", score_gradient, query_slice, preferred_element_type=single_layer
        )
        grad_values = jnp.einsum(
            "pni,pnx->pix",
            attention_probabilities.astype(narrow_slice),
            attention_gradient_slice,
            preferred_element_type=single_layer,
        )
        grad_kv = lax.dynamic_update_slice_in_dim(
            grad_kv, jnp.concatenate([grad_keys, grad_values], -1), block_index * block_len, 1
        )
        return (grad_query, grad_kv)

    grad_query, grad_kv = lax.fori_loop(
        0,
        needed,
        grad_step,
        (
            jnp.zeros((sequences, row_count, HEAD_SIZE), single_layer),
            jnp.zeros((sequences, full_len, 2 * HEAD_SIZE), single_layer),
        ),
    )
    own_kv = lax.psum_scatter(
        grad_kv.astype(jnp.bfloat16), "ctx", scatter_dimension=1, tiled=True
    ).astype(jnp.float32)
    query_back = rotate(
        grad_query.reshape(sequences, tok_count, head_count, HEAD_SIZE),
        cosine[None, :, None],
        -sine_part[None, :, None],
    )
    key_back = rotate(own_kv[..., :HEAD_SIZE], cosine[None], -sine_part[None])
    grad_qkv_low = jnp.concatenate(
        [query_back.reshape(sequences, tok_count, query_width), key_back, own_kv[..., HEAD_SIZE:]],
        -1,
    ).astype(narrow_slice)
    sigmoid_z = jax.nn.sigmoid(z_vals)
    grad_y = grad_mamba * z_vals * sigmoid_z
    grad_z = grad_mamba * mamba_y * silu_slope(z_vals)
    grad_skip = jnp.sum(grad_y * xs_vals, (0, 1, 3))
    grad_xs = grad_y * skip_gain[:, None]
    grad_ssm_low = grad_y.astype(narrow_slice)
    grad_matrix = jnp.einsum(
        "bthp,bshp->bhts", grad_ssm_low, xs_low, preferred_element_type=single_layer
    )
    grad_xs = grad_xs + jnp.einsum(
        "bhts,bthp->bshp", mix_matrix, grad_ssm_low, preferred_element_type=single_layer
    )
    shared = grad_matrix * expo
    grad_pair = jnp.sum(shared * step_heads[:, :, None, :], 1)
    grad_step_heads = jnp.sum(shared * pair[:, None], 2)
    grad_gap = shared * pair[:, None] * step_heads[:, :, None, :]
    grad_cum_heads = jnp.sum(grad_gap, 3) - jnp.sum(grad_gap, 2)
    inter_low = (grad_ssm_low.astype(single_layer) * entry_decay[..., None]).astype(narrow_slice)
    grad_entry = jnp.sum(grad_ssm_low.astype(single_layer) * inter_term, -1)
    grad_c = jnp.einsum("bthp,bhpn->btn", inter_low, state_low, preferred_element_type=single_layer)
    grad_state_in = jnp.einsum(
        "bthp,btn->bhpn", inter_low, c_low, preferred_element_type=single_layer
    )
    carry_gate = (seg_float[:, -1] == seg_before).astype(single_layer)[:, None] * jnp.exp(
        cumulative[:, -1]
    )
    _, later_grad = prefix(
        (carry_gate, grad_state_in),
        "ctx",
        link_grads,
        (jnp.ones_like(carry_gate), jnp.zeros_like(grad_state_in)),
    )
    later_low = later_grad.astype(narrow_slice)
    grad_weighted = jnp.einsum(
        "bhpn,bsn->bshp", later_low, b_low, preferred_element_type=single_layer
    )
    grad_b = jnp.einsum(
        "bshp,bhpn->bsn", weighted_low, later_low, preferred_element_type=single_layer
    )
    grad_xs = grad_xs + grad_weighted * end_weight[..., None]
    grad_end = jnp.sum(grad_weighted * xs_vals, -1)
    grad_log_end = grad_end * end_weight
    grad_cum = jnp.moveaxis(grad_cum_heads, 1, 2) + grad_entry * entry_decay - grad_log_end
    grad_cum = grad_cum.at[:, -1].add(
        carry_gate * jnp.sum(later_grad * state_before, (2, 3)) + jnp.sum(grad_log_end, 1)
    )
    pair_low = grad_pair.astype(narrow_slice)
    grad_c = grad_c + jnp.einsum(
        "bts,bsn->btn", pair_low, b_low, preferred_element_type=single_layer
    )
    grad_b = grad_b + jnp.einsum(
        "bts,btn->bsn", pair_low, c_low, preferred_element_type=single_layer
    )
    grad_log_step = jnp.flip(jnp.cumsum(jnp.flip(grad_cum, 1), 1), 1)
    grad_step = (
        jnp.moveaxis(grad_step_heads, 1, 2) + grad_end * end_decay - grad_log_step * decay_rate
    )
    grad_log_decay = jnp.sum(grad_log_step * log_step, (0, 1))
    grad_raw = grad_step * jax.nn.sigmoid(step_raw + step_bias)
    grad_step_bias = jnp.sum(grad_raw, (0, 1))
    grad_steps = lax.dynamic_update_slice_in_dim(
        jnp.zeros((sequences, tok_count, M_HEADS), single_layer),
        grad_raw,
        tp_index * mamba_count,
        2,
    )
    post_x = grad_xs.reshape(sequences, tok_count, mamba_width) * silu_slope(conv_x_pre)
    post_bc = jnp.concatenate([grad_b, grad_c], -1) * silu_slope(conv_bc_pre)
    next_x, next_bc = shifted((post_x[:, :reach], post_bc[:, :reach]), "ctx", -1)
    grad_in_x, conv_x_w_part, conv_x_b_part = conv_backward(
        jnp.concatenate([post_x, next_x], 1),
        ext_x,
        seg_float,
        seg_before_ext,
        seg_after_ext,
        conv_x_weight,
        tok_count,
    )
    grad_zx_low = jnp.concatenate(
        [grad_z.reshape(sequences, tok_count, mamba_width), grad_in_x], -1
    ).astype(narrow_slice)
    first_part = jnp.einsum(
        "btc,dc->btd", grad_qkv_low, full_qkv, preferred_element_type=single_layer
    )
    first_part = first_part + jnp.einsum(
        "btc,dc->btd", grad_zx_low, full_zx, preferred_element_type=single_layer
    )
    first_sum, bc_total, steps_total = (
        lax.psum(first_part.astype(jnp.bfloat16), "tp").astype(jnp.float32),
        lax.psum(jnp.concatenate([post_bc, next_bc], 1).astype(jnp.bfloat16), "tp").astype(
            jnp.float32
        ),
        lax.psum(grad_steps.astype(jnp.bfloat16), "tp").astype(jnp.float32),
    )
    grad_in_bc, conv_bc_w_part, conv_bc_b_part = conv_backward(
        bc_total, ext_bc, seg_float, seg_before_ext, seg_after_ext, conv_bc_weight, tok_count
    )
    bcd_low = jnp.concatenate([grad_in_bc, steps_total], -1).astype(narrow_slice)
    grad_first = first_sum + jnp.einsum(
        "btc,dc->btd", bcd_low, full_bcd, preferred_element_type=single_layer
    )
    grad_qkv_w = jnp.einsum(
        "btd,btc->dc", first_norm_slice, grad_qkv_low, preferred_element_type=single_layer
    )
    grad_zx_w = jnp.einsum(
        "btd,btc->dc", first_norm_slice, grad_zx_low, preferred_element_type=single_layer
    )
    grad_bcd_w = jnp.einsum(
        "btd,btc->dc", first_norm_slice, bcd_low, preferred_element_type=single_layer
    )
    grad_gain_one = jnp.sum(grad_first * first_normed, (0, 1))
    tokens_grad = grad_middle + norm_back(grad_first, first_normed, first_scale, gain_one)
    qkv_grad, zx_grad, bcd_grad, mix_grad, gu_grad, down_grad, gain_one_grad, gain_two_grad = (
        lax.psum_scatter(grad_qkv_w, ("dp", "ctx"), scatter_dimension=0, tiled=True),
        lax.psum_scatter(grad_zx_w, ("dp", "ctx"), scatter_dimension=0, tiled=True),
        lax.psum_scatter(grad_bcd_w, ("dp", "ctx"), scatter_dimension=0, tiled=True),
        lax.psum_scatter(grad_mix_w, ("dp", "ctx"), scatter_dimension=0, tiled=True),
        lax.psum_scatter(grad_gu_w, ("dp", "ctx"), scatter_dimension=0, tiled=True),
        lax.psum_scatter(grad_down_w, ("dp", "ctx"), scatter_dimension=0, tiled=True),
        lax.psum_scatter(grad_gain_one, ("dp", "ctx"), scatter_dimension=0, tiled=True),
        lax.psum_scatter(grad_gain_two, ("dp", "ctx"), scatter_dimension=0, tiled=True),
    )
    (
        decay_grad,
        bias_grad,
        skip_grad,
        conv_x_w_grad,
        conv_x_b_grad,
        conv_bc_w_grad,
        conv_bc_b_grad,
    ) = lax.psum(
        (
            grad_log_decay,
            grad_step_bias,
            grad_skip,
            conv_x_w_part,
            conv_x_b_part,
            conv_bc_w_part,
            conv_bc_b_part,
        ),
        ("dp", "ctx"),
    )
    return (
        layer_out,
        tokens_grad,
        gain_one_grad,
        gain_two_grad,
        qkv_grad,
        zx_grad,
        bcd_grad,
        mix_grad,
        gu_grad,
        down_grad,
        decay_grad,
        bias_grad,
        skip_grad,
        conv_x_w_grad,
        conv_x_b_grad,
        conv_bc_w_grad,
        conv_bc_b_grad,
    )


def solution(mesh):
    in_specs = (
        P("dp", "ctx", None),
        P("dp", "ctx"),
        P("dp", "ctx", None),
        P(("dp", "ctx")),
        P(("dp", "ctx")),
        P(("dp", "ctx"), "tp"),
        P(("dp", "ctx"), "tp"),
        P(("dp", "ctx"), None),
        P(("dp", "ctx"), "tp"),
        P(("dp", "ctx"), "tp"),
        P(("dp", "ctx"), "tp"),
        P("tp"),
        P("tp"),
        P("tp"),
        P(None, "tp"),
        P("tp"),
        P(),
        P(),
    )
    out_specs = (
        P("dp", "ctx", None),
        P("dp", "ctx", None),
        P(("dp", "ctx")),
        P(("dp", "ctx")),
        P(("dp", "ctx"), "tp"),
        P(("dp", "ctx"), "tp"),
        P(("dp", "ctx"), None),
        P(("dp", "ctx"), "tp"),
        P(("dp", "ctx"), "tp"),
        P(("dp", "ctx"), "tp"),
        P("tp"),
        P("tp"),
        P("tp"),
        P(None, "tp"),
        P("tp"),
        P(),
        P(),
    )
    return jax.shard_map(
        per_device, mesh=mesh, in_specs=in_specs, out_specs=out_specs, check_vma=False
    )
```

profile of v0, /device:TPU:10, one launch (start us, length us, event | category | flops | bytes accessed | tf_op | source)
XLA Modules:
  0.0 1407.3 jit_solution(11259823142755013219)
XLA Ops:
  11.7 31.9 %all-reduce.7 = (bf16[1024]{0:T(1024)(128)(2,1)S(1)}, bf16[1024]{0:T(1024)(128)(2,1)}) all-reduce(bf16[1024]{0:T(1024)(128)(2,1)S(1)} %dynamic-update-slice.3, bf16[1024]{0:T(1024)(128)(2,1)S(1)} %dynamic-update-slice.6), channel_id=1, replica_groups=mesh['dp'=4,'ctx'=4,'tp'=2] {'dp','ctx'}, use_global_device_ids=true, to_apply=%add | all-reduce | flops 2048 | bytes 8192
  45.1 48.7 %all_gather.68 = bf16[1024,280]{1,0:T(8,128)(2,1)S(1)} all-gather(bf16[64,280]{1,0:T(8,128)(2,1)} %param.37), channel_id=1, replica_groups=mesh['dp'=4,'ctx'=4,'tp'=2] {'dp','ctx'}, dimensions={0}, use_global_device_ids=true | all-gather | bytes 609280 | tf_op jit(solution)/shard_map/all_gather | solution.py:180
  94.9 7.1 all_gather.67
  104.2 8.1 all_gather.69
  116.4 5.5 fusion.216
  122.0 7.2 all_gather.66
  134.3 44.1 %all_gather.75 = bf16[1024,384]{1,0:T(8,128)(2,1)S(1)} all-gather(bf16[64,384]{1,0:T(8,128)(2,1)S(1)} %copy-done.70), channel_id=1, replica_groups=mesh['dp'=4,'ctx'=4,'tp'=2] {'dp','ctx'}, dimensions={0}, use_global_device_ids=true | all-gather | bytes 835584 | tf_op jit(solution)/shard_map/all_gather | solution.py:178
  182.8 8.9 all-reduce.8
  192.4 7.1 all_gather.73
  202.5 9.9 all_gather.76
  216.7 5.2 while.69
  236.4 5.3 while.72
  256.2 29.1 %all-reduce.14.cloned.1.call-done = bf16[2,256,1024]{2,1,0:T(8,128)(2,1)} async-done(((bf16[2,256,1024]{2,1,0:T(8,128)(2,1)}), bf16[2,256,1024]{2,1,0:T(8,128)(2,1)}) %all-reduce.14.cloned.1.call-update) | async-done | bytes 1048592 | tf_op jit(solution)/shard_map/psum | solution.py:377
  287.1 78.2 %all-gather.15.cloned.1.call-done = bf16[1024,2048]{1,0:T(8,128)(2,1)} async-done(((bf16[64,2048]{1,0:T(8,128)(2,1)}), bf16[1024,2048]{1,0:T(8,128)(2,1)}) %all-gather.15.cloned.1.call-update) | async-done | bytes 4194320 | tf_op jit(solution)/shard_map/all_gather | solution.py:182
  365.3 6.7 fusion.70
  372.0 55.6 %all-gather.17.cloned.1.call-done = bf16[1024,1024]{1,0:T(8,128)(2,1)} async-done(((bf16[64,1024]{1,0:T(8,128)(2,1)}), bf16[1024,1024]{1,0:T(8,128)(2,1)}) %all-gather.17.cloned.1.call-update) | async-done | bytes 2097168 | tf_op jit(solution)/shard_map/all_gather | solution.py:183
  427.6 6.2 multiply_convert_fusion.4
  442.5 7.2 all_gather.83
  449.6 7.7 all-reduce.16.cloned.1.call-done
  467.0 15.2 %while.71 = (s32[]{:T(128)}, f32[2,1024,64]{1,2,0:T(8,128)S(1)}, bf16[2,1024,128]{2,1,0:T(8,128)(2,1)}, s32[]{:T(128)}, bf16[2,1024]{1,0:T(2,128)(2,1)S(1)}, /*i...) while((s32[]{:T(128)}, f32[2,1024,64]{1,2,0:T(8,128)S(1)}, ...), condition=%wide.region_18.19_spmd.clone, body=%wide.region_17.18_spmd.clone.sunk | while | flops 690104832 | bytes 41644316 | solution.py:455
  513.1 5.2 multiply_reduce_fusion.1
  527.4 29.2 %all-gather.21.cloned.1.call-done = bf16[8,12,64,128]{3,2,1,0:T(8,128)(2,1)} async-done(((bf16[2,12,64,128]{3,2,1,0:T(8,128)(2,1)}), bf16[8,12,64,128]{3,2,1,0:T(8,128)(2,1)}) %all-gather.21.cloned.1.call-update) | async-done | bytes 1572880 | tf_op jit(solution)/shard_map/all_gather | solution.py:47
  601.4 11.3 all-reduce.18.cloned.1.call-done
  624.3 5.4 copy.342
  641.8 7.4 convolution_bitcast_fusion
  656.0 65.4 %all-reduce.6 = (f32[1024]{0:T(1024)S(1)}, f32[1024]{0:T(1024)S(1)}, f32[12]{0:T(128)}, f32[12]{0:T(128)}, f32[12]{0:T(128)}, /*index=5*/f32[4,768]{1,0:T(4,128)...) all-reduce(f32[1024]{0:T(1024)S(1)} %get-tuple-element.772, ...), channel_id=7, replica_groups=mesh['dp'=4,'ctx'=4,'tp'=2] {'dp','ctx'}, use_global_device_ids=true, to_apply=%region_37.38.clone | all-reduce | flops 7204 | bytes 57632
  727.1 16.1 %reduce-scatter.12.cloned.1.call-done = f32[64,384]{1,0:T(8,128)} async-done(((f32[1024,384]{1,0:T(8,128)}), f32[64,384]{1,0:T(8,128)}) %reduce-scatter.12.cloned.1.call-update) | async-done | bytes 98320 | tf_op jit(solution)/shard_map/reduce_scatter | solution.py:590
  743.3 128.7 %reduce-scatter.16.cloned.1.call-done = f32[64,280]{1,0:T(8,128)} async-done(((f32[1024,280]{1,0:T(8,128)}), f32[64,280]{1,0:T(8,128)}) %reduce-scatter.16.cloned.1.call-update) | async-done | bytes 71696 | tf_op jit(solution)/shard_map/reduce_scatter | solution.py:592
  872.0 96.8 %reduce-scatter.22.cloned.1.call-done = f32[64,1024]{1,0:T(8,128)} async-done(((f32[1024,1024]{1,0:T(8,128)}), f32[64,1024]{1,0:T(8,128)}) %reduce-scatter.22.cloned.1.call-update) | async-done | bytes 262160
  968.8 97.5 %reduce-scatter.18.cloned.1.call-done = f32[64,1024]{1,0:T(8,128)} async-done(((f32[1024,1024]{1,0:T(8,128)}), f32[64,1024]{1,0:T(8,128)}) %reduce-scatter.18.cloned.1.call-update) | async-done | bytes 262160 | tf_op jit(solution)/shard_map/reduce_scatter | solution.py:593
  1066.3 150.9 %reduce-scatter.14.cloned.1.call-done = f32[64,1536]{1,0:T(8,128)} async-done(((f32[1024,1536]{1,0:T(8,128)}), f32[64,1536]{1,0:T(8,128)}) %reduce-scatter.14.cloned.1.call-update) | async-done | bytes 393232 | tf_op jit(solution)/shard_map/reduce_scatter | solution.py:591
  1217.2 183.2 %reduce-scatter.20.cloned.1.call-done = f32[64,2048]{1,0:T(8,128)} async-done(((f32[1024,2048]{1,0:T(8,128)}), f32[64,2048]{1,0:T(8,128)}) %reduce-scatter.20.cloned.1.call-update) | async-done | bytes 524304 | tf_op jit(solution)/shard_map/reduce_scatter | solution.py:594
  (582 shorter events, 228.2 us)
Async XLA Ops:
  7.2 86.6 %copy-start.5 = (bf16[2,256,1024]{2,1,0:T(8,128)(2,1)S(1)}, bf16[2,256,1024]{2,1,0:T(8,128)(2,1)}, u32[]{:S(2)}) copy-start(bf16[2,256,1024]{2,1,0:T(8,128)(2,1)} %param.30) | copy-start | bytes 3145732
  7.2 109.2 %all-gather.11.cloned.1.call-start = ((), (), s32[]{:S(2)}) async-start(), calls=%async_computation.7 | async-start | bytes 3342336 | tf_op jit(solution)/shard_map/all_gather | solution.py:179
  7.9 228.5 %all-gather.19.cloned.1.call-start = ((), (), s32[]{:S(2)}) async-start(), calls=%async_computation.19 | async-start | bytes 1966080 | tf_op jit(solution)/shard_map/all_gather | solution.py:22
  43.5 134.9 %copy-start.101 = (f32[1024]{0:T(1024)}, f32[1024]{0:T(1024)S(1)}, u32[]{:S(2)}) copy-start(f32[1024]{0:T(1024)S(1)} %convert_element_type.341) | copy-start | bytes 12292
  45.0 133.4 %copy-start.122 = (f32[2,256]{1,0:T(2,128)}, f32[2,256]{1,0:T(2,128)S(1)}, u32[]{:S(2)}) copy-start(f32[2,256]{1,0:T(2,128)S(1)} %add_rsqrt_fusion.1) | copy-start | bytes 6148
  45.0 49.8 %copy-start.99 = (s32[2,256]{1,0:T(2,128)S(1)}, s32[2,256]{1,0:T(2,128)}, u32[]{:S(2)}) copy-start(s32[2,256]{1,0:T(2,128)} %param.31) | copy-start | bytes 6148
  45.1 56.9 %copy-start.144 = (f32[12]{0:T(128)S(1)}, f32[12]{0:T(128)}, u32[]{:S(2)}) copy-start(f32[12]{0:T(128)} %param.41) | copy-start | bytes 148
  45.1 57.4 %copy-start.128 = (f32[12]{0:T(128)S(1)}, f32[12]{0:T(128)}, u32[]{:S(2)}) copy-start(f32[12]{0:T(128)} %param.42) | copy-start | bytes 148
  131.8 46.6 %copy-start.13 = (bf16[2,256,768]{2,1,0:T(8,128)(2,1)}, bf16[2,256,768]{2,1,0:T(8,128)(2,1)S(1)}, u32[]{:S(2)}) copy-start(bf16[2,256,768]{2,1,0:T(8,128)(2,1)S(1)} %get-tuple-element.899) | copy-start | bytes 2359300
  133.3 117.1 %all-gather.13.cloned.1.call-start = ((), (), s32[]{:S(2)}) async-start(), calls=%async_computation.8 | async-start | bytes 2228224 | tf_op jit(solution)/shard_map/all_gather | solution.py:181
  134.0 151.3 %all-reduce.14.cloned.1.call-start = ((), (), s32[]{:S(2)}) async-start(), calls=%async_computation.9 | async-start | bytes 2097152 | tf_op jit(solution)/shard_map/psum | solution.py:377
  181.0 32.5 %slice-start = ((f32[2,256,384]{2,1,0:T(8,128)}), f32[2,256,256]{2,1,0:T(8,128)S(1)}, s32[]{:S(2)}) async-start(f32[2,256,384]{2,1,0:T(8,128)} %copy-done.28), calls=%async_computation.23 | async-start | bytes 1048576 | tf_op jit(solution)/shard_map/slice | solution.py:210
  254.5 110.8 %all-gather.15.cloned.1.call-start = ((), (), s32[]{:S(2)}) async-start(), calls=%async_computation.10 | async-start | bytes 4456448 | tf_op jit(solution)/shard_map/all_gather | solution.py:182
  255.1 172.4 %all-gather.17.cloned.1.call-start = ((), (), s32[]{:S(2)}) async-start(), calls=%async_computation.11 | async-start | bytes 2228224 | tf_op jit(solution)/shard_map/all_gather | solution.py:183
  255.7 201.6 %all-reduce.16.cloned.1.call-start = ((), (), s32[]{:S(2)}) async-start(), calls=%async_computation.12 | async-start | bytes 2097152 | tf_op jit(solution)/shard_map/psum | solution.py:406
  256.2 204.1 %copy-start.59 = (f32[1024]{0:T(1024)}, f32[1024]{0:T(1024)S(1)}, u32[]{:S(2)}) copy-start(f32[1024]{0:T(1024)S(1)} %convert_element_type.372) | copy-start | bytes 12292
  285.3 80.0 %copy-start.8 = (bf16[2,256,1024]{2,1,0:T(8,128)(2,1)S(1)}, bf16[2,256,1024]{2,1,0:T(8,128)(2,1)}, u32[]{:S(2)}) copy-start(bf16[2,256,1024]{2,1,0:T(8,128)(2,1)} %all-reduce.14.cloned.1.call-done) | copy-start | bytes 3145732
  287.1 173.2 %copy-start.79 = (f32[2,256]{1,0:T(2,128)}, f32[2,256]{1,0:T(2,128)S(1)}, u32[]{:S(2)}) copy-start(f32[2,256]{1,0:T(2,128)S(1)} %add_rsqrt_fusion) | copy-start | bytes 6148
  438.5 84.5 %reduce-scatter.10.cloned.1.call-start = ((), (), s32[]{:S(2)}) async-start(), calls=%async_computation.13 | async-start | bytes 655360 | tf_op jit(solution)/shard_map/reduce_scatter | solution.py:464
  482.2 74.4 %all-gather.21.cloned.1.call-start = ((), (), s32[]{:S(2)}) async-start(), calls=%async_computation.20 | async-start | bytes 1966080 | tf_op jit(solution)/shard_map/all_gather | solution.py:47
  496.1 116.6 %all-reduce.18.cloned.1.call-start = ((), (), s32[]{:S(2)}) async-start(), calls=%async_computation.22 | async-start | bytes 4980736 | tf_op jit(solution)/shard_map/psum | solution.py:390
  571.0 9.4 collective-permute-start.1
  578.4 6.7 collective-permute-start
  590.2 153.0 %reduce-scatter.12.cloned.1.call-start = ((), (), s32[]{:S(2)}) async-start(), calls=%async_computation.14 | async-start | bytes 1671168 | tf_op jit(solution)/shard_map/reduce_scatter | solution.py:590
  593.6 278.4 %reduce-scatter.16.cloned.1.call-start = ((), (), s32[]{:S(2)}) async-start(), calls=%async_computation.16 | async-start | bytes 1671168 | tf_op jit(solution)/shard_map/reduce_scatter | solution.py:592
  594.9 22.7 %copy-start.103 = (f32[1024]{0:T(1024)S(1)}, f32[1024]{0:T(1024)}, u32[]{:S(2)}) copy-start(f32[1024]{0:T(1024)} %copy-done.101) | copy-start | bytes 12292
  595.0 22.7 %copy-start.124 = (f32[2,256]{1,0:T(2,128)S(1)}, f32[2,256]{1,0:T(2,128)}, u32[]{:S(2)}) copy-start(f32[2,256]{1,0:T(2,128)} %copy-done.122) | copy-start | bytes 6148
  619.8 349.0 %reduce-scatter.22.cloned.1.call-start = ((), (), s32[]{:S(2)}) async-start(), calls=%async_computation.21 | async-start | bytes 4456448
  629.8 436.5 %reduce-scatter.18.cloned.1.call-start = ((), (), s32[]{:S(2)}) async-start(), calls=%async_computation.17 | async-start | bytes 4456448 | tf_op jit(solution)/shard_map/reduce_scatter | solution.py:593
  634.6 582.6 %reduce-scatter.14.cloned.1.call-start = ((), (), s32[]{:S(2)}) async-start(), calls=%async_computation.15 | async-start | bytes 6684672 | tf_op jit(solution)/shard_map/reduce_scatter | solution.py:591
  640.6 759.7 %reduce-scatter.20.cloned.1.call-start = ((), (), s32[]{:S(2)}) async-start(), calls=%async_computation.18 | async-start | bytes 8912896 | tf_op jit(solution)/shard_map/reduce_scatter | solution.py:594
  652.3 70.3 %copy-start.88 = (f32[2,256]{1,0:T(2,128)S(1)}, f32[2,256]{1,0:T(2,128)}, u32[]{:S(2)}) copy-start(f32[2,256]{1,0:T(2,128)} %copy-done.87) | copy-start | bytes 6148
  (138 other events, 847.8 us)
Sparse Core Ops, SparseCore 0:
  10.8 73.5 all-gather.10
  133.4 38.9 all-gather.18
  175.2 62.0 all-gather.12
  254.7 30.6 all-reduce.13
  288.3 76.9 all-gather.14
  368.3 59.1 all-gather.16
  438.6 18.6 all-reduce.15
  482.3 40.6 reduce-scatter.9
  525.6 30.9 all-gather.20
  590.3 22.3 all-reduce.17
  618.1 125.1 reduce-scatter.11
  748.5 123.4 reduce-scatter.15
  874.9 93.8 reduce-scatter.21
  971.5 94.7 reduce-scatter.17
  1071.9 145.1 reduce-scatter.13
  1219.9 180.3 reduce-scatter.19
where the time goes:
time: 1420 us; the launch traced here: 1410 us
  waiting for transfers between devices  894 us (63%)
  blocking collectives  249 us (18%)
  matrix products  105 us (7%)
  other arithmetic  66.7 us (5%)
  local copies, waits for them, and re-layouts  66.5 us (5%)
  between operations  18.6 us (1%)
    reduce_scatter x1, waiting for transfers between devices, per_device(): lax.psum_scatter(grad_gu_w, ('dp', 'ctx'), scatter_dimension=0, tiled=True)  183 us
    reduce_scatter x1, waiting for transfers between devices, per_device(): lax.psum_scatter(grad_zx_w, ('dp', 'ctx'), scatter_dimension=0, tiled=True)  151 us
    reduce_scatter x1, waiting for transfers between devices, per_device(): lax.psum_scatter(grad_bcd_w, ('dp', 'ctx'), scatter_dimension=0, tiled=True)  129 us
    unnamed x3, blocking collectives  106 us
    unnamed x17, waiting for transfers between devices  99.4 us
    reduce_scatter x1, waiting for transfers between devices, per_device(): lax.psum_scatter(grad_mix_w, ('dp', 'ctx'), scatter_dimension=0, tiled=True)  97.5 us
    all_gather x1, waiting for transfers between devices, per_device(): lax.all_gather(gate_up_weight, ('dp', 'ctx'), axis=0, tiled=True)  78.2 us
    all_gather x1, waiting for transfers between devices, per_device(): lax.all_gather(down_weight_matrix, ('dp', 'ctx'), axis=0, tiled=True)  55.6 us
  transfers between devices with their start and end apart: 18, of which 14 were waited for; matrix products, arithmetic and copies ran while one was open for 11% of the time, Pallas kernels for 0%

commit v1 on v0

--- a/solution.py
+++ b/solution.py
@@ -66,6 +66,25 @@
     count = lax.axis_size(axis)
     initial, last = (max(0, -steps), min(count, count - steps))
     return lax.ppermute(value, axis, [(source, source + steps) for source in range(initial, last)])
+
+
+def pair_sum(partial):
+    low = partial.astype(jnp.bfloat16)
+    if lax.axis_size("tp") != 2:
+        return lax.psum(low, "tp").astype(jnp.float32)
+    other = lax.ppermute(low, "tp", [(0, 1), (1, 0)])
+    return low.astype(jnp.float32) + other.astype(jnp.float32)
+
+
+def gather_rows(*shards):
+    return [lax.all_gather(shard, ("dp", "ctx"), axis=0, tiled=True) for shard in shards]
+
+
+def scatter_rows(*partials):
+    return [
+        lax.psum_scatter(part, ("dp", "ctx"), scatter_dimension=0, tiled=True).astype(jnp.float32)
+        for part in partials
+    ]
 
 
 def rms_scale(values):
@@ -174,18 +193,30 @@
     row_count = tok_count * head_count
     score_scale = HEAD_SIZE ** (-0.5)
     reach = conv_x_weight.shape[0] - 1
-    full_qkv, full_zx, full_bcd, full_mix, full_gu, full_down, gain_one, gain_two = (
-        lax.all_gather(attention_input_weight, ("dp", "ctx"), axis=0, tiled=True),
-        lax.all_gather(state_space_input_weight, ("dp", "ctx"), axis=0, tiled=True),
-        lax.all_gather(scan_input_weight, ("dp", "ctx"), axis=0, tiled=True),
-        lax.all_gather(mixer_output_weight, ("dp", "ctx"), axis=0, tiled=True),
-        lax.all_gather(gate_up_weight, ("dp", "ctx"), axis=0, tiled=True),
-        lax.all_gather(down_weight_matrix, ("dp", "ctx"), axis=0, tiled=True),
-        lax.all_gather(attn_gain, ("dp", "ctx"), axis=0, tiled=True),
-        lax.all_gather(ffn_gain, ("dp", "ctx"), axis=0, tiled=True),
-    )
-    gain_one = gain_one.astype(single_layer)
-    gain_two = gain_two.astype(single_layer)
+    qkv_width = attention_input_weight.shape[1]
+    zx_width = state_space_input_weight.shape[1]
+    bcd_width = scan_input_weight.shape[1]
+    first_pad = -(qkv_width + zx_width + bcd_width + 2) % 128
+    first_shard = jnp.concatenate(
+        [
+            state_space_input_weight,
+            attention_input_weight,
+            scan_input_weight,
+            attn_gain[:, None],
+            ffn_gain[:, None],
+            jnp.zeros((attn_gain.shape[0], first_pad), narrow_slice),
+        ],
+        1,
+    )
+    full_first, full_mix, full_gu, full_down = gather_rows(
+        first_shard, mixer_output_weight, gate_up_weight, down_weight_matrix
+    )
+    first_width = qkv_width + zx_width + bcd_width
+    full_zx = full_first[:, :zx_width]
+    full_qkv = full_first[:, zx_width : zx_width + qkv_width]
+    full_bcd = full_first[:, zx_width + qkv_width : first_width]
+    gain_one = full_first[:, first_width].astype(single_layer)
+    gain_two = full_first[:, first_width + 1].astype(single_layer)
     layer_inputs = tokens.astype(single_layer)
     first_scale = rms_scale(layer_inputs)
     first_normed = layer_inputs * first_scale
@@ -374,7 +405,7 @@
         [mamba_out.reshape(sequences, tok_count, mamba_width).astype(narrow_slice), attn_low], -1
     )
     mix_part = jnp.einsum("btc,dc->btd", mixer_slice, full_mix, preferred_element_type=single_layer)
-    middle_state = layer_inputs + lax.psum(mix_part.astype(jnp.bfloat16), "tp").astype(jnp.float32)
+    middle_state = layer_inputs + pair_sum(mix_part)
     second_scale = rms_scale(middle_state)
     second_normed = middle_state * second_scale
     second_norm_slice = (second_normed * gain_two).astype(narrow_slice)
@@ -386,9 +417,7 @@
     ffn_part = jnp.einsum(
         "btc,dc->btd", activation_slice, full_down, preferred_element_type=single_layer
     )
-    layer_out = (
-        middle_state + lax.psum(ffn_part.astype(jnp.bfloat16), "tp").astype(jnp.float32)
-    ).astype(narrow_slice)
+    layer_out = (middle_state + pair_sum(ffn_part)).astype(narrow_slice)
     cotangent = out_grad.astype(single_layer)
     grad_down_w = jnp.einsum(
         "btd,btc->dc", out_grad, activation_slice, preferred_element_type=single_layer
@@ -403,7 +432,7 @@
     second_part = jnp.einsum(
         "btc,dc->btd", grad_gu_low, full_gu, preferred_element_type=single_layer
     )
-    grad_second = lax.psum(second_part.astype(jnp.bfloat16), "tp").astype(jnp.float32)
+    grad_second = pair_sum(second_part)
     grad_gain_two = jnp.sum(grad_second * second_normed, (0, 1))
     grad_middle = cotangent + norm_back(grad_second, second_normed, second_scale, gain_two)
     grad_mix_low = grad_middle.astype(narrow_slice)
@@ -562,11 +591,9 @@
         "btc,dc->btd", grad_zx_low, full_zx, preferred_element_type=single_layer
     )
     first_sum, bc_total, steps_total = (
-        lax.psum(first_part.astype(jnp.bfloat16), "tp").astype(jnp.float32),
-        lax.psum(jnp.concatenate([post_bc, next_bc], 1).astype(jnp.bfloat16), "tp").astype(
-            jnp.float32
-        ),
-        lax.psum(grad_steps.astype(jnp.bfloat16), "tp").astype(jnp.float32),
+        pair_sum(first_part),
+        pair_sum(jnp.concatenate([post_bc, next_bc], 1)),
+        pair_sum(grad_steps),
     )
     grad_in_bc, conv_bc_w_part, conv_bc_b_part = conv_backward(
         bc_total, ext_bc, seg_float, seg_before_ext, seg_after_ext, conv_bc_weight, tok_count
@@ -586,16 +613,46 @@
     )
     grad_gain_one = jnp.sum(grad_first * first_normed, (0, 1))
     tokens_grad = grad_middle + norm_back(grad_first, first_normed, first_scale, gain_one)
-    qkv_grad, zx_grad, bcd_grad, mix_grad, gu_grad, down_grad, gain_one_grad, gain_two_grad = (
-        lax.psum_scatter(grad_qkv_w, ("dp", "ctx"), scatter_dimension=0, tiled=True),
-        lax.psum_scatter(grad_zx_w, ("dp", "ctx"), scatter_dimension=0, tiled=True),
-        lax.psum_scatter(grad_bcd_w, ("dp", "ctx"), scatter_dimension=0, tiled=True),
-        lax.psum_scatter(grad_mix_w, ("dp", "ctx"), scatter_dimension=0, tiled=True),
-        lax.psum_scatter(grad_gu_w, ("dp", "ctx"), scatter_dimension=0, tiled=True),
-        lax.psum_scatter(grad_down_w, ("dp", "ctx"), scatter_dimension=0, tiled=True),
-        lax.psum_scatter(grad_gain_one, ("dp", "ctx"), scatter_dimension=0, tiled=True),
-        lax.psum_scatter(grad_gain_two, ("dp", "ctx"), scatter_dimension=0, tiled=True),
-    )
+    grad_first_w = jnp.concatenate(
+        [
+            grad_zx_w.astype(narrow_slice),
+            grad_qkv_w.astype(narrow_slice),
+            grad_bcd_w.astype(narrow_slice),
+            grad_gain_one.astype(narrow_slice)[:, None],
+            grad_gain_two.astype(narrow_slice)[:, None],
+            jnp.zeros((model_width, first_pad), narrow_slice),
+        ],
+        1,
+    )
+    first_own, mix_grad, gu_grad, down_grad = scatter_rows(
+        grad_first_w,
+        grad_mix_w.astype(narrow_slice),
+        grad_gu_w.astype(narrow_slice),
+        grad_down_w.astype(narrow_slice),
+    )
+    zx_grad = first_own[:, :zx_width]
+    qkv_grad = first_own[:, zx_width : zx_width + qkv_width]
+    bcd_grad = first_own[:, zx_width + qkv_width : first_width]
+    gain_one_grad = first_own[:, first_width]
+    gain_two_grad = first_own[:, first_width + 1]
+    small_parts = (
+        grad_log_decay,
+        grad_step_bias,
+        grad_skip,
+        conv_x_w_part,
+        conv_x_b_part,
+        conv_bc_w_part,
+        conv_bc_b_part,
+    )
+    flat = jnp.concatenate([part.reshape(-1) for part in small_parts])
+    small_count = flat.shape[0]
+    flat = jnp.pad(flat, (0, -small_count % 1024)).reshape(-1, 128)
+    small_total = lax.psum(flat, ("dp", "ctx")).reshape(-1)
+    small_sums = []
+    start = 0
+    for part in small_parts:
+        small_sums.append(small_total[start : start + part.size].reshape(part.shape))
+        start += part.size
     (
         decay_grad,
         bias_grad,
@@ -604,18 +661,7 @@
         conv_x_b_grad,
         conv_bc_w_grad,
         conv_bc_b_grad,
-    ) = lax.psum(
-        (
-            grad_log_decay,
-            grad_step_bias,
-            grad_skip,
-            conv_x_w_part,
-            conv_x_b_part,
-            conv_bc_w_part,
-            conv_bc_b_part,
-        ),
-        ("dp", "ctx"),
-    )
+    ) = small_sums
     return (
         layer_out,
         tokens_grad,

time: 1420 us -> 908 us (0.64)
  waiting for transfers between devices: 894 us -> 480 us
  blocking collectives: 249 us -> 139 us
    reduce_scatter x5 -> x3, waiting for transfers between devices: 576 us -> 254 us  [scatter_rows(): lax.psum_scatter(part, ('dp', 'ctx'), scatter_dimension=0, tiled=True)]
    unnamed x3 -> x1, blocking collectives: 106 us -> 8.12 us
    unnamed x17 -> x12, waiting for transfers between devices: 99.4 us -> 1.87 us
    all_gather x2 -> x0, blocking collectives: 92.8 us -> none  [the longest x1 48.7 us: per_device(): lax.all_gather(scan_input_weight, ('dp', 'ctx'), axis=0, tiled=True)]
    all_gather x4, waiting for transfers between devices: 134 us -> 217 us  [gather_rows(): lax.all_gather(shard, ('dp', 'ctx'), axis=0, tiled=True)]
    psum x1, blocking collectives: 3.42 us -> 62.8 us  [per_device(): small_total = lax.psum(flat, ('dp', 'ctx')).reshape(-1)]
    psum x3 -> x0, waiting for transfers between devices: 48.1 us -> none  [the longest x1 29.1 us: per_device(): lax.psum(mix_part.astype(jnp.bfloat16), 'tp').astype(jnp.float32)]
    all_gather x1, waiting for transfers between devices: 29.2 us -> 0.02 us  [prefix(): lax.all_gather(a.astype(kind), axis)]
  transfers between devices with their start and end apart: 18 -> 19, of which waited for: 14 -> 9; matrix products, arithmetic and copies ran while one was open for 11% -> 20% of each run, Pallas kernels for 0% -> 0%
where the time goes in v1:
time: 908 us; the launch traced here: 896 us
  waiting for transfers between devices  480 us (53%)
  blocking collectives  139 us (15%)
  matrix products  102 us (11%)
  local copies, waits for them, and re-layouts  78.7 us (9%)
  other arithmetic  70.2 us (8%)
  between operations  17.2 us (2%)
    reduce_scatter x3, waiting for transfers between devices, scatter_rows(): lax.psum_scatter(part, ('dp', 'ctx'), scatter_dimension=0, tiled=True)  254 us
    all_gather x4, waiting for transfers between devices, gather_rows(): lax.all_gather(shard, ('dp', 'ctx'), axis=0, tiled=True)  217 us
    psum x1, blocking collectives, per_device(): small_total = lax.psum(flat, ('dp', 'ctx')).reshape(-1)  62.8 us
    all_gather x1, blocking collectives, prefix(): lax.all_gather(a.astype(kind), axis)  25.2 us
    unnamed x297, local copies, waits for them, and re-layouts  21 us
  transfers between devices with their start and end apart: 19, of which 9 were waited for; matrix products, arithmetic and copies ran while one was open for 20% of the time, Pallas kernels for 0%

profile of v1, /device:TPU:10, one launch (start us, length us, event | category | flops | bytes accessed | tf_op | source)
XLA Modules:
  0.0 896.0 jit_solution(14839092426956883734)
XLA Ops:
  11.4 8.1 all_gather.54
  24.1 68.9 %all-gather.11.cloned.1.call-done = bf16[1024,2304]{1,0:T(8,128)(2,1)} async-done(((bf16[64,2304]{1,0:T(8,128)(2,1)}), bf16[1024,2304]{1,0:T(8,128)(2,1)}) %all-gather.11.cloned.1.call-update) | async-done | bytes 4718608 | tf_op jit(solution)/shard_map/all_gather | solution.py:80
  94.5 5.4 fusion.208
  102.7 7.3 all_gather.53
  113.0 8.1 all_gather.55
  132.4 8.1 all-reduce.3
  148.4 8.3 all_gather.59
  162.3 11.2 %all_gather.61 = bf16[2,1024,128]{2,1,0:T(8,128)(2,1)S(1)} all-gather(bf16[2,256,128]{2,1,0:T(8,128)(2,1)S(1)} %pad_maximum_fusion.18), channel_id=1, replica_groups=mesh['dp'=4,'ctx'=4,'tp'=2] {'ctx'}, dimensions={1}, use_global_device_ids=true | all-gather | bytes 655360 | tf_op jit(solution)/shard_map/all_gather | solution.py:256
  175.9 5.2 while.69
  181.2 3.9 while.70
  186.5 7.8 while.72
  196.3 3.8 multiply_convert_fusion.8
  200.4 21.9 %all-gather.13.cloned.1.call-done = bf16[1024,1024]{1,0:T(8,128)(2,1)} async-done(((bf16[64,1024]{1,0:T(8,128)(2,1)}), bf16[1024,1024]{1,0:T(8,128)(2,1)}) %all-gather.13.cloned.1.call-update) | async-done | bytes 2097168 | tf_op jit(solution)/shard_map/all_gather | solution.py:80
  228.7 71.2 %all-gather.15.cloned.1.call-done = bf16[1024,2048]{1,0:T(8,128)(2,1)} async-done(((bf16[64,2048]{1,0:T(8,128)(2,1)}), bf16[1024,2048]{1,0:T(8,128)(2,1)}) %all-gather.15.cloned.1.call-update) | async-done | bytes 4194320 | tf_op jit(solution)/shard_map/all_gather | solution.py:80
  299.9 6.7 fusion.70
  306.5 55.2 %all-gather.17.cloned.1.call-done = bf16[1024,1024]{1,0:T(8,128)(2,1)} async-done(((bf16[64,1024]{1,0:T(8,128)(2,1)}), bf16[1024,1024]{1,0:T(8,128)(2,1)}) %all-gather.17.cloned.1.call-update) | async-done | bytes 2097168 | tf_op jit(solution)/shard_map/all_gather | solution.py:80
  361.7 5.2 multiply_convert_fusion.4
  378.5 4.4 multiply_add_fusion.1
  388.7 17.9 %while.71 = (s32[]{:T(128)}, f32[2,1024,64]{1,2,0:T(8,128)}, bf16[2,1024,128]{2,1,0:T(8,128)(2,1)}, s32[]{:T(128)}, bf16[2,1024]{1,0:T(2,128)(2,1)S(1)}, /*index...) while((s32[]{:T(128)}, f32[2,1024,64]{1,2,0:T(8,128)}, ...), condition=%wide.region_15.16_spmd.clone, body=%wide.region_14.15_spmd.clone.sunk | while | flops 690104832 | bytes 45838692 | solution.py:484
  394.0 4.9 fusion.271
  411.5 4.8 fusion.99
  430.3 25.2 %all_gather.67 = bf16[4,2,12]{2,1,0:T(2,128)(2,1)S(1)} all-gather(bf16[1,2,12]{2,1,0:T(2,128)(2,1)S(1)} %fusion.177), channel_id=1, replica_groups=mesh['dp'=4,'ctx'=4,'tp'=2] {'ctx'}, dimensions={0}, use_global_device_ids=true | all-gather | bytes 240 | tf_op jit(solution)/shard_map/all_gather | solution.py:47
  455.5 6.1 bitcast_convert_fusion.1
  463.1 6.2 multiply_reduce_fusion.1
  500.1 4.6 collective-permute-start.5
  538.2 4.9 fusion.85
  543.4 7.7 concatenate.90
  553.2 62.8 %psum.7 = f32[6144]{0:T(1024)S(1)} all-reduce(f32[6144]{0:T(1024)S(1)} %pad.6), channel_id=1, replica_groups=mesh['dp'=4,'ctx'=4,'tp'=2] {'dp','ctx'}, use_global_device_ids=true, to_apply=%region_50.51 | all-reduce | flops 6144 | bytes 49152 | tf_op jit(solution)/shard_map/psum | solution.py:650
  621.1 4.1 fusion.84
  625.2 10.3 %reduce-scatter.12.cloned.1.call-done = bf16[64,1024]{1,0:T(8,128)(2,1)} async-done(((bf16[1024,1024]{1,0:T(8,128)(2,1)}), bf16[64,1024]{1,0:T(8,128)(2,1)}) %reduce-scatter.12.cloned.1.call-update) | async-done | bytes 131088 | tf_op jit(solution)/shard_map/reduce_scatter | solution.py:85
  637.2 102.3 %reduce-scatter.14.cloned.1.call-done = bf16[64,2048]{1,0:T(8,128)(2,1)} async-done(((bf16[1024,2048]{1,0:T(8,128)(2,1)}), bf16[64,2048]{1,0:T(8,128)(2,1)}) %reduce-scatter.14.cloned.1.call-update) | async-done | bytes 262160 | tf_op jit(solution)/shard_map/reduce_scatter | solution.py:85
  741.3 141.5 %reduce-scatter.10.cloned.1.call-done = bf16[64,2304]{1,0:T(8,128)(2,1)} async-done(((bf16[1024,2304]{1,0:T(8,128)(2,1)}), bf16[64,2304]{1,0:T(8,128)(2,1)}) %reduce-scatter.10.cloned.1.call-update) | async-done | bytes 294928 | tf_op jit(solution)/shard_map/reduce_scatter | solution.py:85
  (586 shorter events, 201.6 us)
Async XLA Ops:
  7.2 85.8 %all-gather.11.cloned.1.call-start = ((), (), s32[]{:S(2)}) async-start(), calls=%async_computation.5 | async-start | bytes 5013504 | tf_op jit(solution)/shard_map/all_gather | solution.py:80
  10.7 175.8 %all-gather.19.cloned.1.call-start = ((), (), s32[]{:S(2)}) async-start(), calls=%async_computation.13 | async-start | bytes 1966080 | tf_op jit(solution)/shard_map/all_gather | solution.py:22
  21.2 89.0 %copy-start.67 = (f32[768]{0:T(1024)}, f32[768]{0:T(1024)S(1)}, u32[]{:S(2)}) copy-start(f32[768]{0:T(1024)S(1)} %get-tuple-element.786) | copy-start | bytes 9220
  23.2 98.1 %copy-start.121 = (f32[12]{0:T(128)}, f32[12]{0:T(128)S(1)}, u32[]{:S(2)}) copy-start(f32[12]{0:T(128)S(1)} %get-tuple-element.944) | copy-start | bytes 148
  23.3 100.9 %copy-start.80 = (f32[2,256]{1,0:T(2,128)}, f32[2,256]{1,0:T(2,128)S(1)}, u32[]{:S(2)}) copy-start(f32[2,256]{1,0:T(2,128)S(1)} %get-tuple-element.936) | copy-start | bytes 6148
  23.3 102.5 %copy-start.59 = (f32[2,256]{1,0:T(2,128)}, f32[2,256]{1,0:T(2,128)S(1)}, u32[]{:S(2)}) copy-start(f32[2,256]{1,0:T(2,128)S(1)} %get-tuple-element.937) | copy-start | bytes 6148
  23.3 102.4 %copy-start.98 = (f32[1,256]{1,0:T(1,128)}, f32[1,256]{1,0:T(1,128)S(1)}, u32[]{:S(2)}) copy-start(f32[1,256]{1,0:T(1,128)S(1)} %get-tuple-element.923) | copy-start | bytes 3076
  23.3 102.4 %copy-start.100 = (f32[1,256]{1,0:T(1,128)}, f32[1,256]{1,0:T(1,128)S(1)}, u32[]{:S(2)}) copy-start(f32[1,256]{1,0:T(1,128)S(1)} %get-tuple-element.924) | copy-start | bytes 3076
  23.4 102.4 %copy-start.102 = (f32[1,256]{1,0:T(1,128)}, f32[1,256]{1,0:T(1,128)S(1)}, u32[]{:S(2)}) copy-start(f32[1,256]{1,0:T(1,128)S(1)} %get-tuple-element.925) | copy-start | bytes 3076
  23.4 102.4 %copy-start.104 = (f32[1,256]{1,0:T(1,128)}, f32[1,256]{1,0:T(1,128)S(1)}, u32[]{:S(2)}) copy-start(f32[1,256]{1,0:T(1,128)S(1)} %get-tuple-element.926) | copy-start | bytes 3076
  24.1 101.8 %copy-start.61 = (f32[2,256]{1,0:T(2,128)}, f32[2,256]{1,0:T(2,128)S(1)}, u32[]{:S(2)}) copy-start(f32[2,256]{1,0:T(2,128)S(1)} %get-tuple-element.933) | copy-start | bytes 6148
  24.1 101.8 %copy-start.63 = (f32[2,256]{1,0:T(2,128)}, f32[2,256]{1,0:T(2,128)S(1)}, u32[]{:S(2)}) copy-start(f32[2,256]{1,0:T(2,128)S(1)} %get-tuple-element.934) | copy-start | bytes 6148
  24.1 101.8 %copy-start.65 = (f32[2,256]{1,0:T(2,128)}, f32[2,256]{1,0:T(2,128)S(1)}, u32[]{:S(2)}) copy-start(f32[2,256]{1,0:T(2,128)S(1)} %get-tuple-element.935) | copy-start | bytes 6148
  128.5 93.8 %all-gather.13.cloned.1.call-start = ((), (), s32[]{:S(2)}) async-start(), calls=%async_computation.6 | async-start | bytes 2228224 | tf_op jit(solution)/shard_map/all_gather | solution.py:80
  129.2 170.6 %all-gather.15.cloned.1.call-start = ((), (), s32[]{:S(2)}) async-start(), calls=%async_computation.7 | async-start | bytes 4456448 | tf_op jit(solution)/shard_map/all_gather | solution.py:80
  129.8 231.9 %all-gather.17.cloned.1.call-start = ((), (), s32[]{:S(2)}) async-start(), calls=%async_computation.8 | async-start | bytes 2228224 | tf_op jit(solution)/shard_map/all_gather | solution.py:80
  130.4 357.0 %reduce-scatter.8.cloned.1.call-start = ((), (), s32[]{:S(2)}) async-start(), calls=%async_computation.9 | async-start | bytes 655360 | tf_op jit(solution)/shard_map/reduce_scatter | solution.py:493
  225.4 2.7 collective-permute-start
  228.7 149.8 %copy-start.6 = (f32[2,256,1024]{2,1,0:T(8,128)}, f32[2,256,1024]{2,1,0:T(8,128)S(1)}, u32[]{:S(2)}) copy-start(f32[2,256,1024]{2,1,0:T(8,128)S(1)} %get-tuple-element.888) | copy-start | bytes 6291460
  228.7 149.8 %copy-start.82 = (f32[2,256]{1,0:T(2,128)}, f32[2,256]{1,0:T(2,128)S(1)}, u32[]{:S(2)}) copy-start(f32[2,256]{1,0:T(2,128)S(1)} %add_rsqrt_fusion) | copy-start | bytes 6148
  370.4 5.2 collective-permute-start.2
  372.6 5.8 collective-permute-start.1
  406.6 87.1 %all-gather.21.cloned.1.call-start = ((), (), s32[]{:S(2)}) async-start(), calls=%async_computation.14 | async-start | bytes 1966080 | tf_op jit(solution)/shard_map/all_gather | solution.py:47
  418.6 200.6 %reduce-scatter.16.cloned.1.call-start = ((), (), s32[]{:S(2)}) async-start(), calls=%async_computation.15 | async-start | bytes 2228224
  424.1 211.5 %reduce-scatter.12.cloned.1.call-start = ((), (), s32[]{:S(2)}) async-start(), calls=%async_computation.11 | async-start | bytes 2228224 | tf_op jit(solution)/shard_map/reduce_scatter | solution.py:85
  429.4 310.1 %reduce-scatter.14.cloned.1.call-start = ((), (), s32[]{:S(2)}) async-start(), calls=%async_computation.12 | async-start | bytes 4456448 | tf_op jit(solution)/shard_map/reduce_scatter | solution.py:85
  461.5 421.2 %reduce-scatter.10.cloned.1.call-start = ((), (), s32[]{:S(2)}) async-start(), calls=%async_computation.10 | async-start | bytes 5013504 | tf_op jit(solution)/shard_map/reduce_scatter | solution.py:85
  500.1 21.6 %collective-permute-start.5 = (bf16[2,3,256]{1,2,0:T(8,128)(2,1)}, bf16[2,3,256]{1,2,0:T(8,128)(2,1)}, u32[]{:S(2)}, u32[]{:S(2)}) collective-permute-start(bf16[2,3,256]{1,2,0:T(8,128)(2,1)} %slice.453), channel_id=1, source_target_pairs={{2,0},{4,2},{6,4},{3,1},{5,3},{7,5},{10,8},{12,10},{14,12},{11,9},... | collective-permute-start | bytes 9224 | tf_op jit(solution)/shard_map/ppermute | solution.py:68
  516.2 19.4 %collective-permute-start.7 = (bf16[2,256,24]{1,2,0:T(8,128)(2,1)S(1)}, bf16[2,256,24]{1,2,0:T(8,128)(2,1)S(1)}, u32[]{:S(2)}, u32[]{:S(2)}) collective-permute-start(bf16[2,256,24]{1,2,0:T(8,128)(2,1)S(1)} %dynamic_update_slice.6), channel_id=1, source_target_pairs={{0,1},{1,0},{2,3},{3,2},{4,5},{5,4},{6,7},{7,6},{8,9},{9,8},{10,11... | collective-permute-start | bytes 73736 | tf_op jit(solution)/shard_map/ppermute | solution.py:75
  519.6 7.3 collective-permute-start.3
  522.6 13.0 %collective-permute-start.6 = (bf16[2,259,256]{1,2,0:T(8,128)(2,1)S(1)}, bf16[2,259,256]{1,2,0:T(8,128)(2,1)S(1)}, u32[]{:S(2)}, u32[]{:S(2)}) collective-permute-start(bf16[2,259,256]{1,2,0:T(8,128)(2,1)S(1)} %pad_maximum_fusion.13), channel_id=1, source_target_pairs={{0,1},{1,0},{2,3},{3,2},{4,5},{5,4},{6,7},{7,6},{8,9},{9,8},{10,11... | collective-permute-start | bytes 795656 | tf_op jit(solution)/shard_map/ppermute | solution.py:75
  531.9 6.4 collective-permute-start.4
  (133 other events, 1513.1 us)
Sparse Core Ops, SparseCore 0:
  11.4 81.5 all-gather.10
  128.6 30.1 all-gather.18
  161.6 60.7 all-gather.12
  225.0 74.8 all-gather.14
  302.5 59.1 all-gather.16
  406.8 41.4 reduce-scatter.7
  450.8 30.9 all-gather.20
  484.2 71.0 reduce-scatter.15
  557.7 77.8 reduce-scatter.11
  637.8 101.6 reduce-scatter.13
  745.5 137.2 reduce-scatter.9

commit v2 on v1

--- a/solution.py
+++ b/solution.py
@@ -208,9 +208,15 @@
         ],
         1,
     )
-    full_first, full_mix, full_gu, full_down = gather_rows(
-        first_shard, mixer_output_weight, gate_up_weight, down_weight_matrix
-    )
+    mix_width = mixer_output_weight.shape[1]
+    gu_end = mix_width + gate_up_weight.shape[1]
+    later_shard = jnp.concatenate(
+        [mixer_output_weight, gate_up_weight, down_weight_matrix], 1
+    )
+    full_first, full_later = gather_rows(first_shard, later_shard)
+    full_mix = full_later[:, :mix_width]
+    full_gu = full_later[:, mix_width:gu_end]
+    full_down = full_later[:, gu_end:]
     first_width = qkv_width + zx_width + bcd_width
     full_zx = full_first[:, :zx_width]
     full_qkv = full_first[:, zx_width : zx_width + qkv_width]
@@ -624,12 +630,18 @@
         ],
         1,
     )
-    first_own, mix_grad, gu_grad, down_grad = scatter_rows(
-        grad_first_w,
-        grad_mix_w.astype(narrow_slice),
-        grad_gu_w.astype(narrow_slice),
-        grad_down_w.astype(narrow_slice),
-    )
+    grad_later_w = jnp.concatenate(
+        [
+            grad_mix_w.astype(narrow_slice),
+            grad_gu_w.astype(narrow_slice),
+            grad_down_w.astype(narrow_slice),
+        ],
+        1,
+    )
+    first_own, later_own = scatter_rows(grad_first_w, grad_later_w)
+    mix_grad = later_own[:, :mix_width]
+    gu_grad = later_own[:, mix_width:gu_end]
+    down_grad = later_own[:, gu_end:]
     zx_grad = first_own[:, :zx_width]
     qkv_grad = first_own[:, zx_width : zx_width + qkv_width]
     bcd_grad = first_own[:, zx_width + qkv_width : first_width]

time: 908 us -> 822 us (0.905)
  waiting for transfers between devices: 480 us -> 412 us
  blocking collectives: 139 us -> 120 us
  matrix products: 102 us -> 90.1 us
  other arithmetic: 70.2 us -> 80.2 us
    all_gather x4 -> x2, waiting for transfers between devices: 217 us -> 145 us  [gather_rows(): lax.all_gather(shard, ('dp', 'ctx'), axis=0, tiled=True)]
    reduce_scatter x3 -> x2, waiting for transfers between devices: 254 us -> 220 us  [scatter_rows(): lax.psum_scatter(part, ('dp', 'ctx'), scatter_dimension=0, tiled=True)]
    all_gather x1, waiting for transfers between devices: 0.02 us -> 26.9 us  [prefix(): lax.all_gather(a.astype(kind), axis)]
    all_gather x1, blocking collectives: 25.2 us -> 7.33 us  [prefix(): lax.all_gather(a.astype(kind), axis)]
    reduce_scatter x1, waiting for transfers between devices: 0.01 us -> 14.6 us  [per_device(): lax.psum_scatter(grad_kv.astype(jnp.bfloat16), 'ctx', scatter_dimension=1...]
    unnamed x297 -> x292, local copies, waits for them, and re-layouts: 21 us -> 12.5 us
  transfers between devices with their start and end apart: 19 -> 15, of which waited for: 9 -> 8; matrix products, arithmetic and copies ran while one was open for 20% -> 20% of each run, Pallas kernels for 0% -> 0%
where the time goes in v2:
time: 822 us; the launch traced here: 811 us
  waiting for transfers between devices  412 us (50%)
  blocking collectives  120 us (15%)
  matrix products  90.1 us (11%)
  local copies, waits for them, and re-layouts  83 us (10%)
  other arithmetic  80.2 us (10%)
  between operations  17.3 us (2%)
    reduce_scatter x2, waiting for transfers between devices, scatter_rows(): lax.psum_scatter(part, ('dp', 'ctx'), scatter_dimension=0, tiled=True)  220 us
    all_gather x2, waiting for transfers between devices, gather_rows(): lax.all_gather(shard, ('dp', 'ctx'), axis=0, tiled=True)  145 us
    psum x1, blocking collectives, per_device(): small_total = lax.psum(flat, ('dp', 'ctx')).reshape(-1)  62.8 us
    all_gather x1, waiting for transfers between devices, prefix(): lax.all_gather(a.astype(kind), axis)  26.9 us
  transfers between devices with their start and end apart: 15, of which 8 were waited for; matrix products, arithmetic and copies ran while one was open for 20% of the time, Pallas kernels for 0%

profile of v2, /device:TPU:10, one launch (start us, length us, event | category | flops | bytes accessed | tf_op | source)
XLA Modules:
  0.0 810.9 jit_solution(11237119126219725836)
XLA Ops:
  11.4 8.1 all_gather.48
  24.1 68.9 %all-gather.9.cloned.1.call-done = bf16[1024,2304]{1,0:T(8,128)(2,1)} async-done(((bf16[64,2304]{1,0:T(8,128)(2,1)}), bf16[1024,2304]{1,0:T(8,128)(2,1)}) %all-gather.9.cloned.1.call-update) | async-done | bytes 4718608 | tf_op jit(solution)/shard_map/all_gather | solution.py:80
  95.0 5.4 fusion.200
  103.3 7.3 all_gather.47
  113.6 8.1 all_gather.49
  133.0 8.1 %all-reduce.3 = (bf16[8]{0:T(256)(128)(2,1)S(1)}, bf16[8]{0:T(256)(128)(2,1)S(1)}) all-reduce(bf16[8]{0:T(256)(128)(2,1)S(1)} %dynamic-update-slice.3, bf16[8]{0:T(256)(128)(2,1)S(1)} %dynamic-update-slice.4), channel_id=2, replica_groups=mesh['dp'=4,'ctx'=4,'tp'=2] {'ctx'}, use_global_device_ids=true, to_apply=%add.1 | all-reduce | flops 16 | bytes 64
  148.4 8.0 all_gather.53
  162.1 9.9 %all_gather.55 = bf16[2,1024,128]{2,1,0:T(8,128)(2,1)S(1)} all-gather(bf16[2,256,128]{2,1,0:T(8,128)(2,1)S(1)} %pad_maximum_fusion.20), channel_id=1, replica_groups=mesh['dp'=4,'ctx'=4,'tp'=2] {'ctx'}, dimensions={1}, use_global_device_ids=true | all-gather | bytes 655360 | tf_op jit(solution)/shard_map/all_gather | solution.py:262
  174.4 5.3 while.69
  179.8 3.9 while.70
  185.5 8.1 while.72
  198.9 75.7 %all-gather.11.cloned.1.call-done = bf16[1024,4096]{1,0:T(8,128)(2,1)} async-done(((bf16[64,4096]{1,0:T(8,128)(2,1)}), bf16[1024,4096]{1,0:T(8,128)(2,1)}) %all-gather.11.cloned.1.call-update) | async-done | bytes 8388624 | tf_op jit(solution)/shard_map/all_gather | solution.py:80
  295.4 7.3 all_gather.59
  305.1 4.2 multiply_add_fusion.1
  309.3 3.6 fusion.91
  317.6 17.8 %while.71 = (s32[]{:T(128)}, f32[2,1024,64]{1,2,0:T(8,128)}, bf16[2,1024,128]{2,1,0:T(8,128)(2,1)}, s32[]{:T(128)}, bf16[2,1024]{1,0:T(2,128)(2,1)S(1)}, /*index...) while((s32[]{:T(128)}, f32[2,1024,64]{1,2,0:T(8,128)}, ...), condition=%wide.region_15.16_spmd.clone, body=%wide.region_14.15_spmd.clone.sunk | while | flops 690104832 | bytes 45838692 | solution.py:490
  317.6 3.7 fusion.261
  322.8 4.8 fusion.263
  340.8 5.3 fusion.96
  357.0 5.2 multiply_reduce_fusion.1
  363.8 14.6 %reduce-scatter.4.cloned.1.call-done = bf16[2,256,128]{2,1,0:T(8,128)(2,1)} async-done(((bf16[2,1024,128]{2,1,0:T(8,128)(2,1)}), bf16[2,256,128]{2,1,0:T(8,128)(2,1)}) %reduce-scatter.4.cloned.1.call-update) | async-done | bytes 131088 | tf_op jit(solution)/shard_map/reduce_scatter | solution.py:499
  385.0 26.9 %all-gather.15.cloned.1.call-done = bf16[8,12,64,128]{3,2,1,0:T(8,128)(2,1)} async-done(((bf16[2,12,64,128]{3,2,1,0:T(8,128)(2,1)}), bf16[8,12,64,128]{3,2,1,0:T(8,128)(2,1)}) %all-gather.15.cloned.1.call-update) | async-done | bytes 1572880 | tf_op jit(solution)/shard_map/all_gather | solution.py:47
  418.4 3.7 collective-permute-start.5
  468.1 4.3 fusion.83
  472.6 7.7 concatenate.97
  480.7 4.3 fusion.90
  485.0 4.5 bitcast_convert_fusion.1
  495.0 6.6 pad_maximum_fusion.1
  503.7 62.8 %psum.7 = f32[6144]{0:T(1024)S(1)} all-reduce(f32[6144]{0:T(1024)S(1)} %pad.6), channel_id=1, replica_groups=mesh['dp'=4,'ctx'=4,'tp'=2] {'dp','ctx'}, use_global_device_ids=true, to_apply=%region_48.49 | all-reduce | flops 6144 | bytes 49152 | tf_op jit(solution)/shard_map/psum | solution.py:662
  569.7 4.1 fusion.82
  573.9 43.9 %reduce-scatter.6.cloned.1.call-done = bf16[64,2304]{1,0:T(8,128)(2,1)} async-done(((bf16[1024,2304]{1,0:T(8,128)(2,1)}), bf16[64,2304]{1,0:T(8,128)(2,1)}) %reduce-scatter.6.cloned.1.call-update) | async-done | bytes 294928 | tf_op jit(solution)/shard_map/reduce_scatter | solution.py:85
  624.1 176.3 %reduce-scatter.8.cloned.1.call-done = bf16[64,4096]{1,0:T(8,128)(2,1)} async-done(((bf16[1024,4096]{1,0:T(8,128)(2,1)}), bf16[64,4096]{1,0:T(8,128)(2,1)}) %reduce-scatter.8.cloned.1.call-update) | async-done | bytes 524304 | tf_op jit(solution)/shard_map/reduce_scatter | solution.py:85
  (572 shorter events, 202.0 us)
Async XLA Ops:
  7.2 87.8 %copy-start.9 = (bf16[2,256,1024]{2,1,0:T(8,128)(2,1)S(1)}, bf16[2,256,1024]{2,1,0:T(8,128)(2,1)}, u32[]{:S(2)}) copy-start(bf16[2,256,1024]{2,1,0:T(8,128)(2,1)} %param.30) | copy-start | bytes 3145732
  7.2 85.8 %all-gather.9.cloned.1.call-start = ((), (), s32[]{:S(2)}) async-start(), calls=%async_computation.3 | async-start | bytes 5013504 | tf_op jit(solution)/shard_map/all_gather | solution.py:80
  10.7 174.8 %all-gather.13.cloned.1.call-start = ((), (), s32[]{:S(2)}) async-start(), calls=%async_computation.8 | async-start | bytes 1966080 | tf_op jit(solution)/shard_map/all_gather | solution.py:22
  20.3 80.2 %copy-start.129 = (f32[2]{0:T(128)}, f32[2]{0:T(128)S(1)}, u32[]{:S(2)}) copy-start(f32[2]{0:T(128)S(1)} %get-tuple-element.708) | copy-start | bytes 28
  21.2 89.6 %copy-start.75 = (f32[768]{0:T(1024)}, f32[768]{0:T(1024)S(1)}, u32[]{:S(2)}) copy-start(f32[768]{0:T(1024)S(1)} %get-tuple-element.701) | copy-start | bytes 9220
  21.2 89.6 %copy-start.77 = (f32[768]{0:T(1024)}, f32[768]{0:T(1024)S(1)}, u32[]{:S(2)}) copy-start(f32[768]{0:T(1024)S(1)} %get-tuple-element.702) | copy-start | bytes 9220
  21.2 89.6 %copy-start.79 = (f32[768]{0:T(1024)}, f32[768]{0:T(1024)S(1)}, u32[]{:S(2)}) copy-start(f32[768]{0:T(1024)S(1)} %get-tuple-element.703) | copy-start | bytes 9220
  21.2 89.6 %copy-start.81 = (f32[768]{0:T(1024)}, f32[768]{0:T(1024)S(1)}, u32[]{:S(2)}) copy-start(f32[768]{0:T(1024)S(1)} %get-tuple-element.704) | copy-start | bytes 9220
  23.3 98.7 %copy-start.124 = (f32[12]{0:T(128)}, f32[12]{0:T(128)S(1)}, u32[]{:S(2)}) copy-start(f32[12]{0:T(128)S(1)} %get-tuple-element.861) | copy-start | bytes 148
  23.4 101.4 %copy-start.88 = (f32[2,256]{1,0:T(2,128)}, f32[2,256]{1,0:T(2,128)S(1)}, u32[]{:S(2)}) copy-start(f32[2,256]{1,0:T(2,128)S(1)} %get-tuple-element.853) | copy-start | bytes 6148
  23.4 103.0 %copy-start.66 = (f32[2,256]{1,0:T(2,128)}, f32[2,256]{1,0:T(2,128)S(1)}, u32[]{:S(2)}) copy-start(f32[2,256]{1,0:T(2,128)S(1)} %get-tuple-element.854) | copy-start | bytes 6148
  23.4 103.0 %copy-start.103 = (f32[1,256]{1,0:T(1,128)}, f32[1,256]{1,0:T(1,128)S(1)}, u32[]{:S(2)}) copy-start(f32[1,256]{1,0:T(1,128)S(1)} %get-tuple-element.840) | copy-start | bytes 3076
  23.4 103.0 %copy-start.105 = (f32[1,256]{1,0:T(1,128)}, f32[1,256]{1,0:T(1,128)S(1)}, u32[]{:S(2)}) copy-start(f32[1,256]{1,0:T(1,128)S(1)} %get-tuple-element.841) | copy-start | bytes 3076
  23.4 103.0 %copy-start.107 = (f32[1,256]{1,0:T(1,128)}, f32[1,256]{1,0:T(1,128)S(1)}, u32[]{:S(2)}) copy-start(f32[1,256]{1,0:T(1,128)S(1)} %get-tuple-element.842) | copy-start | bytes 3076
  23.4 103.0 %copy-start.109 = (f32[1,256]{1,0:T(1,128)}, f32[1,256]{1,0:T(1,128)S(1)}, u32[]{:S(2)}) copy-start(f32[1,256]{1,0:T(1,128)S(1)} %get-tuple-element.843) | copy-start | bytes 3076
  24.1 102.3 %copy-start.69 = (f32[2,256]{1,0:T(2,128)}, f32[2,256]{1,0:T(2,128)S(1)}, u32[]{:S(2)}) copy-start(f32[2,256]{1,0:T(2,128)S(1)} %get-tuple-element.850) | copy-start | bytes 6148
  24.1 102.3 %copy-start.71 = (f32[2,256]{1,0:T(2,128)}, f32[2,256]{1,0:T(2,128)S(1)}, u32[]{:S(2)}) copy-start(f32[2,256]{1,0:T(2,128)S(1)} %get-tuple-element.851) | copy-start | bytes 6148
  24.1 102.3 %copy-start.73 = (f32[2,256]{1,0:T(2,128)}, f32[2,256]{1,0:T(2,128)S(1)}, u32[]{:S(2)}) copy-start(f32[2,256]{1,0:T(2,128)S(1)} %get-tuple-element.852) | copy-start | bytes 6148
  113.5 80.7 %copy-start.17 = (bf16[2,256,768]{1,2,0:T(8,128)(2,1)}, bf16[2,256,768]{1,2,0:T(8,128)(2,1)S(1)}, u32[]{:S(2)}) copy-start(bf16[2,256,768]{1,2,0:T(8,128)(2,1)S(1)} %copy.298) | copy-start | bytes 2359300
  129.1 145.4 %all-gather.11.cloned.1.call-start = ((), (), s32[]{:S(2)}) async-start(), calls=%async_computation.4 | async-start | bytes 8912896 | tf_op jit(solution)/shard_map/all_gather | solution.py:80
  131.0 247.5 %reduce-scatter.4.cloned.1.call-start = ((), (), s32[]{:S(2)}) async-start(), calls=%async_computation.5 | async-start | bytes 655360 | tf_op jit(solution)/shard_map/reduce_scatter | solution.py:499
  277.7 2.7 collective-permute-start
  288.9 13.8 %collective-permute-start.2 = (bf16[2,256,1024]{2,1,0:T(8,128)(2,1)}, bf16[2,256,1024]{2,1,0:T(8,128)(2,1)}, u32[]{:S(2)}, u32[]{:S(2)}) collective-permute-start(bf16[2,256,1024]{2,1,0:T(8,128)(2,1)} %fusion.115), channel_id=1, source_target_pairs={{0,1},{1,0},{2,3},{3,2},{4,5},{5,4},{6,7},{7,6},{8,9},{9,8},{10,11... | collective-permute-start | bytes 3145736 | tf_op jit(solution)/shard_map/ppermute | solution.py:75
  291.3 13.8 %collective-permute-start.1 = (bf16[2,256,1024]{2,1,0:T(8,128)(2,1)}, bf16[2,256,1024]{2,1,0:T(8,128)(2,1)}, u32[]{:S(2)}, u32[]{:S(2)}) collective-permute-start(bf16[2,256,1024]{2,1,0:T(8,128)(2,1)} %fusion.113), channel_id=1, source_target_pairs={{0,1},{1,0},{2,3},{3,2},{4,5},{5,4},{6,7},{7,6},{8,9},{9,8},{10,11... | collective-permute-start | bytes 3145736 | tf_op jit(solution)/shard_map/ppermute | solution.py:75
  335.4 76.4 %all-gather.15.cloned.1.call-start = ((), (), s32[]{:S(2)}) async-start(), calls=%async_computation.9 | async-start | bytes 1966080 | tf_op jit(solution)/shard_map/all_gather | solution.py:47
  347.3 270.4 %reduce-scatter.6.cloned.1.call-start = ((), (), s32[]{:S(2)}) async-start(), calls=%async_computation.6 | async-start | bytes 5013504 | tf_op jit(solution)/shard_map/reduce_scatter | solution.py:85
  418.4 34.0 %collective-permute-start.5 = (bf16[2,3,256]{1,2,0:T(8,128)(2,1)}, bf16[2,3,256]{1,2,0:T(8,128)(2,1)}, u32[]{:S(2)}, u32[]{:S(2)}) collective-permute-start(bf16[2,3,256]{1,2,0:T(8,128)(2,1)} %slice.480), channel_id=1, source_target_pairs={{2,0},{4,2},{6,4},{3,1},{5,3},{7,5},{10,8},{12,10},{14,12},{11,9},... | collective-permute-start | bytes 9224 | tf_op jit(solution)/shard_map/ppermute | solution.py:68
  446.7 18.6 %collective-permute-start.7 = (bf16[2,256,24]{1,2,0:T(8,128)(2,1)S(1)}, bf16[2,256,24]{1,2,0:T(8,128)(2,1)S(1)}, u32[]{:S(2)}, u32[]{:S(2)}) collective-permute-start(bf16[2,256,24]{1,2,0:T(8,128)(2,1)S(1)} %dynamic_update_slice.6), channel_id=1, source_target_pairs={{0,1},{1,0},{2,3},{3,2},{4,5},{5,4},{6,7},{7,6},{8,9},{9,8},{10,11... | collective-permute-start | bytes 73736 | tf_op jit(solution)/shard_map/ppermute | solution.py:75
  449.9 6.8 collective-permute-start.3
  453.3 12.1 %collective-permute-start.6 = (bf16[2,259,256]{1,2,0:T(8,128)(2,1)S(1)}, bf16[2,259,256]{1,2,0:T(8,128)(2,1)S(1)}, u32[]{:S(2)}, u32[]{:S(2)}) collective-permute-start(bf16[2,259,256]{1,2,0:T(8,128)(2,1)S(1)} %pad_maximum_fusion.15), channel_id=1, source_target_pairs={{0,1},{1,0},{2,3},{3,2},{4,5},{5,4},{6,7},{7,6},{8,9},{9,8},{10,11... | collective-permute-start | bytes 795656 | tf_op jit(solution)/shard_map/ppermute | solution.py:75
  461.7 6.4 collective-permute-start.4
  480.4 319.9 %reduce-scatter.8.cloned.1.call-start = ((), (), s32[]{:S(2)}) async-start(), calls=%async_computation.7 | async-start | bytes 8912896 | tf_op jit(solution)/shard_map/reduce_scatter | solution.py:85
  (128 other events, 1018.3 us)
Sparse Core Ops, SparseCore 0:
  11.4 81.5 all-gather.8
  129.3 30.3 all-gather.12
  163.0 111.4 all-gather.10
  335.6 42.8 reduce-scatter.3
  380.9 30.9 all-gather.14
  480.5 137.2 reduce-scatter.5
  620.0 180.2 reduce-scatter.7
